TPU v7x, 512 devices: a whole 4x8x8 slice. The times are simulated.
512 devices in a mesh: row: 64 (over z, y), col: 8 (over x, core).
Axes of the slice: x: 4, y: 8, z: 8, core: 2. Of those that a mesh axis runs over, the one named last changes fastest.
Arguments:
- giant_table: bfloat16 [65536, 128], P('row'), may hold values from -3 to 3
- look_row: int32 [131072], P(('row', 'col')), may hold values from 0 to 1023
- look_owner: int32 [131072, 1], P(('row', 'col')), may hold values from 0 to 63; in each aligned block of 256 rows (0 to 255, 256 to 511, ...) at most 8 rows name the same one
- look_bag: int32 [131072], P(('row', 'col')), may hold values from 0 to 31
- look_count: int32 [512], P(('row', 'col')), may hold values from 128 to 256, as said below
- medium_tables: bfloat16 [15, 256, 512], P(None, None, 'col'), may hold values from -3 to 3
- medium_ids: int32 [16384, 15, 4], P(('row', 'col')), may hold values from 0 to 255
- medium_lengths: int32 [16384, 15], P(('row', 'col')), may hold values from 1 to 4
- dense_features: bfloat16 [16384, 384], P(('row', 'col')), may hold values from -6 to 6
- click_labels: int32 [16384], P(('row', 'col')), may hold values 0 or 1
- cross_left: bfloat16 [8192, 512], P('col'), may hold values from -0.0625 to 0.0625
- cross_right: bfloat16 [512, 8192], P(None, 'col'), may hold values from -0.25 to 0.25
- cross_bias: float32 [8192], P('col'), may hold values from -3 to 3
- top_weight: float32 [8192], P('col'), may hold values from -0.0625 to 0.0625
Outputs:
- sample_grads: bfloat16 [16384, 512], P(('row', 'col'))
- giant_grad: float32 [65536, 128], P('row')
- medium_grad: float32 [15, 256, 512], P(None, None, 'col')
- left_grad: float32 [8192, 512], P(('col', 'row'))
- right_grad: float32 [512, 8192], P('row', 'col')
- bias_grad: float32 [8192], P('col')
- top_grad: float32 [8192], P('col')
Inputs may be any that keep to these rules, and one draw needn't show every extreme that they name: `look_owner`: among the 256 slots of one device at most 8 name the same owner. `look_count`: some device has all 256 slots live.
All inputs are finite; a program needn't handle non-finite values. No bound on the sum of `click_labels` on one device may be relied on, other than what follows from the above.
Results may differ from a plain program's by a relative error of at most 0.015.
Values may be sent and summed in bfloat16 or wider, within the bound.
No kernel may reach another device: no remote copies, remote signals or barrier semaphores. Data moves between devices by JAX's collectives and lax.ppermute only.
A program may use at most 64 MiB of HBM per device.

v0:
```python
import jax
import jax.numpy as jnp
from jax import lax
from jax.sharding import PartitionSpec as P

LOSS_SCALE = 0.015625


def body(
    giant_table,
    look_row,
    look_owner,
    look_bag,
    look_count,
    medium_tables,
    medium_ids,
    medium_lengths,
    dense_features,
    click_labels,
    cross_left,
    cross_right,
    cross_bias,
    top_weight,
):
    row_count = lax.axis_size("row")
    local_batch = dense_features.shape[0]
    lookups = look_row.shape[0]
    giant_width = giant_table.shape[1]
    table_count = medium_tables.shape[0]
    slice_width = medium_tables.shape[2]
    medium_width = table_count * slice_width
    slot_valid = jnp.arange(lookups) < look_count[0]
    valid_float = slot_valid.astype(jnp.float32)[:, None]
    owner_row = look_owner[:, 0]
    looked = giant_table[look_row]
    capacity = 2 * lookups // row_count
    owner_hits = (
        (owner_row[:, None] == jnp.arange(row_count)[None, :]) & slot_valid[:, None]
    ).astype(jnp.int32)
    earlier = jnp.cumsum(owner_hits, axis=0) - owner_hits
    position = jnp.sum(earlier * owner_hits, axis=1)
    target = jnp.where(slot_valid, owner_row * capacity + position, row_count * capacity)
    send_rows = (
        jnp.zeros((row_count * capacity, giant_width), jnp.bfloat16)
        .at[target]
        .set(looked, mode="drop")
    )
    send_bags = (
        jnp.full((row_count * capacity,), local_batch, jnp.int32)
        .at[target]
        .set(look_bag, mode="drop")
    )
    got_rows, got_bags = (
        lax.all_to_all(
            send_rows.reshape(row_count, capacity, giant_width),
            "row",
            split_axis=0,
            concat_axis=0,
            tiled=True,
        ),
        lax.all_to_all(
            send_bags.reshape(row_count, capacity), "row", split_axis=0, concat_axis=0, tiled=True
        ),
    )
    flat_bags = got_bags.reshape(-1)
    pooled = jax.ops.segment_sum(
        got_rows.reshape(-1, giant_width).astype(jnp.float32),
        flat_bags,
        num_segments=local_batch + 1,
    )[:local_batch]
    sample_part = jnp.concatenate([pooled.astype(jnp.bfloat16), dense_features], axis=1)
    host_part = lax.all_to_all(sample_part, "col", split_axis=1, concat_axis=0, tiled=True)
    host_ids, host_lengths, host_labels = (
        lax.all_gather(medium_ids, "col", axis=0, tiled=True),
        lax.all_gather(medium_lengths, "col", axis=0, tiled=True),
        lax.all_gather(click_labels, "col", axis=0, tiled=True),
    )
    host_rows = host_ids.shape[0]
    bag_mask = (jnp.arange(host_ids.shape[2])[None, None, :] < host_lengths[:, :, None]).astype(
        jnp.float32
    )
    looked_medium = jnp.stack(
        [
            medium_tables[table_index][host_ids[:, table_index, :]]
            for table_index in range(table_count)
        ],
        axis=1,
    )
    embedded = jnp.sum(looked_medium.astype(jnp.float32) * bag_mask[..., None], axis=2).astype(
        jnp.bfloat16
    )
    crossed_in = jnp.concatenate([embedded.reshape(host_rows, medium_width), host_part], axis=1)
    inputs_wide = crossed_in.astype(jnp.float32)
    low_rank = lax.psum(
        jnp.dot(crossed_in, cross_left, preferred_element_type=jnp.float32), "col"
    ).astype(jnp.bfloat16)
    expanded = jnp.dot(low_rank, cross_right, preferred_element_type=jnp.float32) + cross_bias
    crossed = inputs_wide * expanded + inputs_wide
    logits = lax.psum(jnp.sum(crossed * top_weight, axis=1), "col")
    residue = (jax.nn.sigmoid(logits) - host_labels.astype(jnp.float32)) * LOSS_SCALE
    grad_crossed = residue[:, None] * top_weight
    grad_expanded = grad_crossed * inputs_wide
    grad_expanded_low = grad_expanded.astype(jnp.bfloat16)
    local_top = jnp.sum(residue[:, None] * crossed, axis=0)
    local_bias = jnp.sum(grad_expanded, axis=0)
    grad_rank = lax.psum(
        lax.dot_general(
            grad_expanded_low,
            cross_right,
            (((1,), (1,)), ((), ())),
            preferred_element_type=jnp.float32,
        ).astype(jnp.bfloat16),
        "col",
    )
    columns = low_rank
    right_grad = lax.psum_scatter(
        lax.dot_general(
            columns, grad_expanded_low, (((0,), (0,)), ((), ())), preferred_element_type=jnp.float32
        ),
        "row",
        scatter_dimension=0,
        tiled=True,
    )
    columns = crossed_in
    left_grad = lax.psum_scatter(
        lax.dot_general(
            columns, grad_rank, (((0,), (0,)), ((), ())), preferred_element_type=jnp.float32
        ),
        "row",
        scatter_dimension=0,
        tiled=True,
    )
    grad_inputs = (
        grad_crossed * (expanded + 1.0)
        + lax.dot_general(
            grad_rank, cross_left, (((1,), (1,)), ((), ())), preferred_element_type=jnp.float32
        )
    ).astype(jnp.bfloat16)
    grad_embedded = (
        grad_inputs[:, :medium_width]
        .reshape(host_rows, table_count, slice_width)
        .astype(jnp.float32)
    )
    table_ids = jnp.broadcast_to(
        jnp.arange(table_count, dtype=jnp.int32)[None, :, None], host_ids.shape
    )
    local_medium = (
        jnp.zeros(medium_tables.shape, jnp.float32)
        .at[table_ids, host_ids]
        .add(grad_embedded[:, :, None, :] * bag_mask[..., None])
    )
    medium_grad, bias_grad, top_grad = lax.psum((local_medium, local_bias, local_top), "row")
    sample_grads = lax.all_to_all(
        grad_inputs[:, medium_width:], "col", split_axis=0, concat_axis=1, tiled=True
    )
    bag_grads = sample_grads[:, :giant_width]
    padded = jnp.concatenate([bag_grads, jnp.zeros((1, giant_width), jnp.bfloat16)], axis=0)
    returned = lax.all_to_all(padded[got_bags], "row", split_axis=0, concat_axis=0, tiled=True)
    slot_grads = returned.reshape(-1, giant_width)[jnp.minimum(target, row_count * capacity - 1)]
    local_giant = jax.ops.segment_sum(
        slot_grads.astype(jnp.float32) * valid_float, look_row, num_segments=giant_table.shape[0]
    )
    giant_grad = lax.psum(local_giant.astype(jnp.bfloat16), "col").astype(jnp.float32)
    return (sample_grads, giant_grad, medium_grad, left_grad, right_grad, bias_grad, top_grad)


def solution(mesh):
    placed = (
        P("row", None),
        P(("row", "col")),
        P(("row", "col"), None),
        P(("row", "col")),
        P(("row", "col")),
        P(None, None, "col"),
        P(("row", "col"), None, None),
        P(("row", "col"), None),
        P(("row", "col"), None),
        P(("row", "col")),
        P("col", None),
        P(None, "col"),
        P("col"),
        P("col"),
    )
    return jax.shard_map(
        body,
        mesh=mesh,
        in_specs=placed,
        out_specs=(
            P(("row", "col"), None),
            P("row", None),
            P(None, None, "col"),
            P(("col", "row"), None),
            P("row", "col"),
            P("col"),
            P("col"),
        ),
        check_vma=False,
    )
```

profile of v0, /device:TPU:1, one launch (start us, length us, event | category | flops | bytes accessed | tf_op | source)
XLA Modules:
  0.0 903.5 jit_solution(2781307178311214745)
XLA Ops:
  13.2 17.1 %all-to-all-start = ((s32[64,1,8]{2,1,0:T(1,128)}), s32[64,1,8]{2,1,0:T(1,128)S(1)}, u32[]{:S(2)}, u32[]{:S(2)}) async-start(s32[64,1,8]{2,1,0:T(1,128)} %bitcast.69), calls=%async_computation | async-start | bytes 65536 | tf_op jit(solution)/shard_map/all_to_all | solution.py:61
  31.2 14.1 %all-gather = s32[8,32,15]{1,2,0:T(8,128)S(1)} all-gather(s32[1,32,15]{1,2,0:T(8,128)} %bitcast.239), channel_id=1, replica_groups=mesh['row'=64,'col'=8] {'col'}, dimensions={0}, use_global_device_ids=true | all-gather | bytes 17280 | tf_op jit(solution)/shard_map/all_gather | solution.py:75
  45.4 13.1 %all_gather.9 = s32[256,15,4]{1,2,0:T(4,128)S(1)} all-gather(s32[32,15,4]{1,2,0:T(4,128)S(1)} %copy.439), channel_id=1, replica_groups=mesh['row'=64,'col'=8] {'col'}, dimensions={0}, use_global_device_ids=true | all-gather | bytes 69120 | tf_op jit(solution)/shard_map/all_gather | solution.py:74
  61.4 2.9 fusion
  64.3 6.8 fusion.37
  92.7 3.2 gather_fusion
  96.8 3.2 gather_fusion.14
  100.1 3.2 gather_fusion.10
  103.3 3.2 gather_fusion.8
  106.5 4.3 gather_fusion.6
  110.8 4.3 gather_fusion.4
  115.0 4.3 gather_fusion.2
  119.3 3.2 gather_fusion.12
  122.5 4.3 gather_fusion.13
  126.8 4.3 gather_fusion.9
  131.1 4.3 gather_fusion.7
  135.3 4.3 gather_fusion.5
  139.6 4.3 gather_fusion.3
  143.8 4.3 gather_fusion.1
  148.1 4.3 gather_fusion.11
  152.4 1.9 constant_dynamic-update-slice_fusion.13
  165.9 1.8 constant_dynamic-update-slice_fusion.5
  172.0 22.3 %multiply_reduce_fusion = bf16[256,15,64]{2,1,0:T(8,128)(2,1)S(1)} fusion(bf16[256,15,4,64]{3,2,1,0:T(4,128)(2,1)} %constant_dynamic-update-slice_fusion, f32[256,15,4]{2,1,0:T(8,128)S(1)} %copy-done.1), kind=kLoop, calls=%fused_computation.23 | loop fusion | flops 2703360 | bytes 2519040 | tf_op jit(solution)/shard_map/reduce_sum | solution.py:89
  194.4 3.7 scatter_custom_fusion.1
  198.2 12.9 %all-to-all-start.1 = ((bf16[64,8,128]{2,1,0:T(8,128)(2,1)}), bf16[64,8,128]{2,1,0:T(8,128)(2,1)S(1)}, u32[]{:S(2)}, u32[]{:S(2)}) async-start(bf16[64,8,128]{2,1,0:T(8,128)(2,1)} %bitcast.70), calls=%async_computation.1 | async-start | bytes 262144 | tf_op jit(solution)/shard_map/all_to_all | solution.py:54
  212.9 9.8 %all-to-all-done.1 = bf16[64,8,128]{2,1,0:T(8,128)(2,1)S(1)} async-done(((bf16[64,8,128]{2,1,0:T(8,128)(2,1)}), bf16[64,8,128]{2,1,0:T(8,128)(2,1)S(1)}, u32[]{:S(2)}, u32[]{:S(2)}) %all-to-all-start.1) | async-done | bytes 131104 | tf_op jit(solution)/shard_map/all_to_all | solution.py:54
  222.7 3.4 scatter_custom_fusion.2
  227.0 5.3 all-to-all-start.2
  235.6 7.6 all-reduce.1
  245.1 27.6 %all-reduce.15 = bf16[256,512]{1,0:T(8,128)(2,1)S(1)} all-reduce(f32[256,512]{1,0:T(8,128)S(1)} %fusion.36), channel_id=1, replica_groups=mesh['row'=64,'col'=8] {'col'}, use_global_device_ids=true, to_apply=%region_7.8 | all-reduce | flops 131072 | bytes 786432 | tf_op jit(solution)/shard_map/psum | solution.py:94
  273.4 15.4 %psum.50 = f32[256]{0:T(256)S(1)} all-reduce(f32[256]{0:T(256)S(1)} %get-tuple-element.94), channel_id=1, replica_groups=mesh['row'=64,'col'=8] {'col'}, use_global_device_ids=true, to_apply=%region_9.10 | all-reduce | flops 256 | bytes 2048 | tf_op jit(solution)/shard_map/psum | solution.py:99
  291.0 57.5 %all-reduce.10.cloned.1.call-done = bf16[256,512]{1,0:T(8,128)(2,1)} async-done(((bf16[256,512]{1,0:T(8,128)(2,1)}), bf16[256,512]{1,0:T(8,128)(2,1)}) %all-reduce.10.cloned.1.call-update) | async-done | bytes 262160 | tf_op jit(solution)/shard_map/psum | solution.py:106
  351.9 6.2 all-to-all-start.3
  358.1 2.0 copy.513
  363.9 1.9 gather_fusion.15
  365.8 13.3 %all-to-all-start.4 = ((bf16[64,8,128]{2,1,0:T(8,128)(2,1)}), bf16[64,8,128]{2,1,0:T(8,128)(2,1)}, u32[]{:S(2)}, u32[]{:S(2)}) async-start(bf16[64,8,128]{2,1,0:T(8,128)(2,1)} %bitcast.78), calls=%async_computation.4 | async-start | bytes 262144 | tf_op jit(solution)/shard_map/all_to_all | solution.py:158
  379.2 3.2 fusion.11
  382.4 1.8 slice.200
  384.2 3.1 copy.514
  387.3 3.2 all-to-all-done.4
  390.5 5.2 scatter_custom_fusion.3
  397.6 8.1 broadcast_multiply_fusion
  405.7 82.7 %scatter_custom_fusion.4 = f32[3840,64]{1,0:T(8,128)S(1)} fusion(s32[15360]{0:T(1024)} %reshape.723, f32[15360,64]{1,0:T(8,128)} %bitcast.207, f32[]{:T(128)} %constant.16.clone.1), kind=kCustom, calls=%fused_computation.39 | custom fusion | flops 983040 | bytes 983552
  490.3 2.7 fusion.35
  495.5 115.0 %all-reduce.3 = (f32[1024]{0:T(1024)}, f32[1024]{0:T(1024)}) all-reduce(f32[1024]{0:T(1024)S(1)} %get-tuple-element.57, f32[1024]{0:T(1024)S(1)} %get-tuple-element.56), channel_id=1, replica_groups=mesh['row'=64,'col'=8] {'row'}, use_global_device_ids=true, to_apply=%region_18.19 | all-reduce | flops 2048 | bytes 16384 | tf_op jit(solution)/shard_map/psum | solution.py:152
  612.3 39.3 %all-reduce.14.cloned.1.call-done = (f32[15,256,64]{1,0,2:T(8,128)}, f32[512,1024]{1,0:T(8,128)}) async-done(((f32[15,256,64]{1,0,2:T(8,128)}, f32[512,1024]{1,0:T(8,128)}), (f32[15,256,64]{1,0,2:T(8,128)}, f32[512,1024]{1,0:T(8,128)})) %all-reduce.14.cloned.1.call-update) | async-done | bytes 3080208 | tf_op jit(solution)/shard_map/psum | solution.py:152
  651.6 2.7 copy.516
  655.7 241.0 %reduce-scatter.2.cloned.1.call-done = f32[16,512]{1,0:T(8,128)} async-done(((f32[1024,512]{1,0:T(8,128)}), f32[16,512]{1,0:T(8,128)}) %reduce-scatter.2.cloned.1.call-update) | async-done | bytes 32784 | tf_op jit(solution)/shard_map/reduce_scatter | solution.py:125
  (205 shorter events, 73.0 us)
Async XLA Ops:
  7.2 265.5 %copy-start = (bf16[512,1024]{1,0:T(8,128)(2,1)S(1)}, bf16[512,1024]{1,0:T(8,128)(2,1)}, u32[]{:S(2)}) copy-start(bf16[512,1024]{1,0:T(8,128)(2,1)} %param.25) | copy-start | bytes 3145732
  13.2 181.1 %all-to-all-start = ((s32[64,1,8]{2,1,0:T(1,128)}), s32[64,1,8]{2,1,0:T(1,128)S(1)}, u32[]{:S(2)}, u32[]{:S(2)}) async-start(s32[64,1,8]{2,1,0:T(1,128)} %bitcast.69), calls=%async_computation | async-start | bytes 65536 | tf_op jit(solution)/shard_map/all_to_all | solution.py:61
  148.1 22.2 %copy-start.8 = (bf16[1024,64]{1,0:T(8,128)(2,1)S(1)}, bf16[1024,64]{1,0:T(8,128)(2,1)}, u32[]{:S(2)}) copy-start(bf16[1024,64]{1,0:T(8,128)(2,1)} %gather_fusion.13) | copy-start | bytes 393220
  152.4 16.2 %copy-start.9 = (bf16[1024,64]{1,0:T(8,128)(2,1)S(1)}, bf16[1024,64]{1,0:T(8,128)(2,1)}, u32[]{:S(2)}) copy-start(bf16[1024,64]{1,0:T(8,128)(2,1)} %gather_fusion.11) | copy-start | bytes 393220
  152.4 19.6 %copy-start.1 = (f32[256,15,4]{2,1,0:T(8,128)S(1)}, f32[256,15,4]{2,1,0:T(8,128)}, u32[]{:S(2)}) copy-start(f32[256,15,4]{2,1,0:T(8,128)} %fusion) | copy-start | bytes 184324
  171.1 23.1 %copy-start.13 = (s32[256]{0:T(256)S(1)}, s32[256]{0:T(256)}, u32[]{:S(2)}) copy-start(s32[256]{0:T(256)} %param.15) | copy-start | bytes 3076
  171.9 39.5 %copy-start.15 = (s32[2]{0:T(128)S(1)}, s32[2]{0:T(128)}, u32[]{:S(2)}) copy-start(s32[2]{0:T(128)} %constant.56) | copy-start | bytes 28
  171.9 54.2 %copy-start.12 = (bf16[32,384]{1,0:T(8,128)(2,1)S(1)}, bf16[32,384]{1,0:T(8,128)(2,1)}, u32[]{:S(2)}) copy-start(bf16[32,384]{1,0:T(8,128)(2,1)} %param.22) | copy-start | bytes 73732
  172.0 60.4 %copy-start.14 = (s32[2]{0:T(128)S(1)}, s32[2]{0:T(128)}, u32[]{:S(2)}) copy-start(s32[2]{0:T(128)} %constant.53) | copy-start | bytes 28
  194.3 41.0 %copy-start.17 = (s32[32]{0:T(128)S(1)}, s32[32]{0:T(128)}, u32[]{:S(2)}) copy-start(s32[32]{0:T(128)} %param.23) | copy-start | bytes 388
  198.2 24.6 %all-to-all-start.1 = ((bf16[64,8,128]{2,1,0:T(8,128)(2,1)}), bf16[64,8,128]{2,1,0:T(8,128)(2,1)S(1)}, u32[]{:S(2)}, u32[]{:S(2)}) async-start(bf16[64,8,128]{2,1,0:T(8,128)(2,1)} %bitcast.70), calls=%async_computation.1 | async-start | bytes 262144 | tf_op jit(solution)/shard_map/all_to_all | solution.py:54
  211.1 61.6 %copy-start.11 = (f32[1024]{0:T(1024)S(1)}, f32[1024]{0:T(1024)}, u32[]{:S(2)}) copy-start(f32[1024]{0:T(1024)} %param.27) | copy-start | bytes 12292
  211.1 61.6 %copy-start.16 = (f32[1024]{0:T(1024)S(1)}, f32[1024]{0:T(1024)}, u32[]{:S(2)}) copy-start(f32[1024]{0:T(1024)} %param.26) | copy-start | bytes 12292
  227.0 16.1 %all-to-all-start.2 = ((bf16[8,2,1024]{2,1,0:T(2,128)(2,1)}), bf16[8,2,1024]{2,1,0:T(2,128)(2,1)S(1)}, u32[]{:S(2)}, u32[]{:S(2)}) async-start(bf16[8,2,1024]{2,1,0:T(2,128)(2,1)} %reshape.803), calls=%async_computation.2 | async-start | bytes 65536 | tf_op jit(solution)/shard_map/all_to_all | solution.py:72
  232.4 116.1 %all-reduce.10.cloned.1.call-start = ((), (), s32[]{:S(2)}) async-start(), calls=%async_computation.6 | async-start | bytes 524288 | tf_op jit(solution)/shard_map/psum | solution.py:106
  233.3 57.0 %copy-start.3 = (bf16[256,15,64]{0,2,1:T(8,128)(2,1)}, bf16[256,15,64]{0,2,1:T(8,128)(2,1)S(1)}, u32[]{:S(2)}) copy-start(bf16[256,15,64]{0,2,1:T(8,128)(2,1)S(1)} %copy.501) | copy-start | bytes 1474564
  273.4 84.7 %copy-start.5 = (f32[256,1024]{0,1:T(8,128)}, f32[256,1024]{0,1:T(8,128)S(1)}, u32[]{:S(2)}) copy-start(f32[256,1024]{0,1:T(8,128)S(1)} %get-tuple-element.95) | copy-start | bytes 3145732
  350.2 0.8 copy-start.7
  351.9 11.0 %all-to-all-start.3 = ((bf16[8,2,1024]{2,1,0:T(2,128)(2,1)}), bf16[8,2,1024]{2,1,0:T(2,128)(2,1)}, u32[]{:S(2)}, u32[]{:S(2)}) async-start(bf16[8,2,1024]{2,1,0:T(2,128)(2,1)} %reshape.805), calls=%async_computation.3 | async-start | bytes 65536 | tf_op jit(solution)/shard_map/all_to_all | solution.py:153
  363.9 23.4 %copy-start.10 = (bf16[32,512]{1,0:T(8,128)(2,1)}, bf16[32,512]{1,0:T(8,128)(2,1)S(1)}, u32[]{:S(2)}) copy-start(bf16[32,512]{1,0:T(8,128)(2,1)S(1)} %all_to_all.52) | copy-start | bytes 98308
  365.8 24.7 %all-to-all-start.4 = ((bf16[64,8,128]{2,1,0:T(8,128)(2,1)}), bf16[64,8,128]{2,1,0:T(8,128)(2,1)}, u32[]{:S(2)}, u32[]{:S(2)}) async-start(bf16[64,8,128]{2,1,0:T(8,128)(2,1)} %bitcast.78), calls=%async_computation.4 | async-start | bytes 262144 | tf_op jit(solution)/shard_map/all_to_all | solution.py:158
  379.1 18.5 %copy-start.2 = (f32[256,15,4]{2,1,0:T(8,128)S(1)}, f32[256,15,4]{2,1,0:T(8,128)}, u32[]{:S(2)}) copy-start(f32[256,15,4]{2,1,0:T(8,128)} %fusion) | copy-start | bytes 184324
  379.1 231.4 %all-reduce.12.cloned.1.call-start = ((), (), s32[]{:S(2)}) async-start(), calls=%async_computation.7 | async-start | bytes 524288 | tf_op jit(solution)/shard_map/psum | solution.py:163
  397.5 254.1 %all-reduce.14.cloned.1.call-start = ((), (), s32[]{:S(2)}) async-start(), calls=%async_computation.9 | async-start | bytes 6291456 | tf_op jit(solution)/shard_map/psum | solution.py:152
  405.7 84.5 %copy-start.4 = (bf16[256,15,64]{0,2,1:T(8,128)(2,1)S(1)}, bf16[256,15,64]{0,2,1:T(8,128)(2,1)}, u32[]{:S(2)}) copy-start(bf16[256,15,64]{0,2,1:T(8,128)(2,1)} %copy-done.3) | copy-start | bytes 1474564
  490.2 4.8 copy-start.6
  490.2 406.5 %reduce-scatter.2.cloned.1.call-start = ((), (), s32[]{:S(2)}) async-start(), calls=%async_computation.8 | async-start | bytes 2129920 | tf_op jit(solution)/shard_map/reduce_scatter | solution.py:125
Sparse Core Ops, SparseCore 0:
  290.4 57.9 all-reduce.9
  397.7 66.6 all-reduce.11
  490.3 161.2 all-reduce.13
  656.1 240.5 reduce-scatter.1
where the time goes:
time: 913 us; the launch traced here: 904 us
  waiting for transfers between devices  352 us (39%)
  blocking collectives  193 us (21%)
  local copies, waits for them, and re-layouts  141 us (15%)
  other arithmetic  134 us (15%)
  starting transfers between devices  54.9 us (6%)
  between operations  16.9 us (2%)
  matrix products  11.5 us (1%)
    reduce_scatter x1, waiting for transfers between devices, body(): lax.psum_scatter(lax.dot_general(columns, grad_rank, (((0,), (0,)), ((),...  241 us
    psum x1, blocking collectives, body(): lax.psum((local_medium, local_bias, local_top), 'row')  115 us
    unnamed x4, other arithmetic  83.6 us
    gather x15, local copies, waits for them, and re-layouts, body(): medium_tables[table_index][host_ids[:, table_index, :]]  58.7 us
    psum x1, waiting for transfers between devices, body(): lax.psum(lax.dot_general(grad_expanded_low, cross_right, (((1,), (1,)), (...  57.5 us
    unnamed x92, local copies, waits for them, and re-layouts  51.9 us
    psum x1, waiting for transfers between devices, body(): lax.psum((local_medium, local_bias, local_top), 'row')  39.3 us
    psum x1, blocking collectives, body(): lax.psum(jnp.dot(crossed_in, cross_left, preferred_element_type=jnp.float...  27.6 us
  transfers between devices with their start and end apart: 9, of which 6 were waited for; matrix products, arithmetic and copies ran while one was open for 28% of the time, Pallas kernels for 0%

commit v1 on v0

v1 whole, which is shorter than its diff:
```python
import functools

import jax
import jax.numpy as jnp
from jax import lax
from jax.experimental import pallas as pl
from jax.experimental.pallas import tpu as pltpu
from jax.sharding import PartitionSpec as P

LOSS_SCALE = 0.015625
F32, BF16, I32 = jnp.float32, jnp.bfloat16, jnp.int32
ROWS, COLS = 64, 8
SIDE = 8
BATCH, HOST = 32, 256
SLOTS, CAP = 256, 8
WIDE, RANK = 1024, 512
TABLES, NAMES, SLICE = 15, 256, 64
BLOCK = 128

NN = ((1,), (0,))
NT = ((1,), (1,))
TN = ((0,), (0,))


def dot(left, right, dims):
    return lax.dot_general(left, right, (dims, ((), ())), preferred_element_type=F32)


def lanes(shape):
    return lax.broadcasted_iota(I32, shape, len(shape) - 1)


def subs(shape):
    return lax.broadcasted_iota(I32, shape, len(shape) - 2)


def one_hot(mask):
    return jnp.where(mask, 1.0, 0.0).astype(BF16)


def call(kernel, outs, *args, smem=(), scratch=()):
    return pl.pallas_call(
        kernel,
        out_shape=outs,
        in_specs=[
            pl.BlockSpec(memory_space=pltpu.SMEM if i in smem else pltpu.VMEM)
            for i in range(len(args))
        ],
        out_specs=jax.tree.map(lambda _: pl.BlockSpec(memory_space=pltpu.VMEM), outs),
        scratch_shapes=list(scratch),
        compiler_params=pltpu.CompilerParams(vmem_limit_bytes=48 * 2**20),
    )(*args)


def struct(shape, dtype):
    return jax.ShapeDtypeStruct(shape, dtype)


def route_kernel(count_ref, row_ref, owner_ref, bag_ref, table_ref, send_ref, names_ref):
    eye = subs((SLOTS, SLOTS)) == lanes((SLOTS, SLOTS))

    def column(ref):
        return jnp.sum(jnp.where(eye, ref[...].astype(F32), 0.0), axis=1, keepdims=True)

    row, bag = column(row_ref), column(bag_ref)
    owner = owner_ref[...]
    live = subs((SLOTS, BLOCK)) < count_ref[0]
    hits = jnp.where((owner == lanes((SLOTS, BLOCK))) & live, 1.0, 0.0)
    before = one_hot(subs((SLOTS, SLOTS)) > lanes((SLOTS, SLOTS)))
    earlier = dot(before, hits.astype(BF16), NN)
    place = jnp.sum(earlier * hits, axis=1, keepdims=True)
    alive = jnp.sum(hits, axis=1, keepdims=True)
    target = jnp.where(alive > 0.5, owner.astype(F32) * CAP + place, -1.0)
    at = target == lanes((SLOTS, ROWS * CAP)).astype(F32)
    looked = dot(one_hot(row == lanes((SLOTS, 1024)).astype(F32)), table_ref[...], NN)
    both = jnp.concatenate(
        [looked.astype(BF16), jnp.broadcast_to(bag, (SLOTS, BLOCK)).astype(BF16)], axis=1
    )
    sent = dot(one_hot(at), both, TN)
    send_ref[...] = jnp.concatenate(
        [
            sent[:, :BLOCK].reshape(ROWS, CAP, BLOCK),
            sent[:, BLOCK:].reshape(ROWS, CAP, BLOCK),
        ],
        axis=1,
    ).astype(BF16)
    named = jnp.sum(jnp.where(at, row + 1.0, 0.0), axis=0, keepdims=True)
    high = jnp.floor(named * (1.0 / 32.0))
    low = named - 32.0 * high
    names_ref[...] = jnp.concatenate(
        [part[:, i * BLOCK : (i + 1) * BLOCK] for part in (high, low) for i in range(4)], axis=0
    )


def pool_kernel(got_ref, dense_ref, ids_ref, names_ref, out_ref):
    got = got_ref[...].astype(F32)
    data = got[:, :CAP].reshape(ROWS * CAP, BLOCK).astype(BF16)
    bags = got[:, CAP:].reshape(ROWS * CAP, BLOCK)
    hot = one_hot(bags == lanes((ROWS * CAP, BLOCK)).astype(F32))
    pooled = dot(hot, data, TN)[:BATCH].astype(BF16).astype(F32)
    eye = subs((BLOCK, BLOCK)) == lanes((BLOCK, BLOCK))
    bag_rows = [
        jnp.sum(jnp.where(eye, bags[i * BLOCK : (i + 1) * BLOCK], 0.0), axis=0, keepdims=True)
        for i in range(4)
    ]
    meta = jnp.concatenate(bag_rows + [names_ref[...], jnp.zeros((4, BLOCK), F32)], axis=0)
    part = jnp.concatenate([pooled, dense_ref[...].astype(F32)], axis=1)
    ids = ids_ref[...].astype(F32)
    for c in range(COLS):
        top = jnp.concatenate([part[:, c * SLICE : (c + 1) * SLICE], ids], axis=1)
        out_ref[c] = jnp.concatenate([top, meta], axis=0).astype(BF16)


def cross_kernel(
    got_ref, tables_ref, left_ref, right_ref, weight_ref, bias_ref, out_ref, x_ref, counts_ref
):
    ids = got_ref[:, :BATCH, SLICE:].astype(F32).reshape(HOST, SLICE)
    part = got_ref[:, :BATCH, :SLICE].astype(F32).reshape(HOST, SLICE)
    name = lanes((HOST, NAMES)).astype(F32)
    pieces = []
    for t in range(TABLES):
        count = jnp.zeros((HOST, NAMES), F32)
        for j in range(4):
            count += jnp.where(ids[:, 4 * t + j : 4 * t + j + 1] == name, 1.0, 0.0)
        low = count.astype(BF16)
        counts_ref[t] = low
        pieces.append(dot(low, tables_ref[t], NN))
        if t % 2:
            x_ref[:, (t // 2) * BLOCK : (t // 2 + 1) * BLOCK] = jnp.concatenate(
                pieces, axis=1
            ).astype(BF16)
            pieces = []
    x_ref[:, WIDE - BLOCK :] = jnp.concatenate(pieces + [part], axis=1).astype(BF16)
    low_rank = jnp.zeros((HOST, RANK), F32)
    back = jnp.zeros((HOST, RANK), F32)
    plain = jnp.zeros((HOST, 1), F32)
    for n in range(4):
        cols = slice(n * 256, (n + 1) * 256)
        x = x_ref[:, cols]
        weighted = x.astype(F32) * weight_ref[:, cols]
        low_rank += dot(x, left_ref[cols, :], NN)
        back += dot(weighted.astype(BF16), right_ref[:, cols], NT)
        plain += jnp.sum(weighted * (bias_ref[:, cols] + 1.0), axis=1, keepdims=True)
    high = plain.astype(BF16).astype(F32)
    lane = lanes((HOST, BLOCK))
    rest = jnp.where(lane == 0, high, jnp.where(lane == 1, plain - high, 0.0))
    out_ref[:, :, :RANK] = low_rank.astype(BF16).reshape(COLS, BATCH, RANK)
    out_ref[:, :, RANK : 2 * RANK] = back.astype(BF16).reshape(COLS, BATCH, RANK)
    out_ref[:, :, 2 * RANK :] = rest.astype(BF16).reshape(COLS, BATCH, BLOCK)


def residue_kernel(got_ref, label_ref, out_ref):
    total = got_ref[0].astype(F32)
    for c in range(1, COLS):
        total += got_ref[c].astype(F32)
    low_rank = total[:, :RANK].astype(BF16).astype(F32)
    back = total[:, RANK : 2 * RANK]
    plain = total[:, 2 * RANK : 2 * RANK + 1] + total[:, 2 * RANK + 1 : 2 * RANK + 2]
    logits = jnp.sum(low_rank * back, axis=1, keepdims=True) + plain
    residue = (jax.nn.sigmoid(logits) - label_ref[...].astype(F32)) * LOSS_SCALE
    high = residue.astype(BF16).astype(F32)
    lane = lanes((BATCH, BLOCK))
    rest = jnp.where(lane == 0, high, jnp.where(lane == 1, residue - high, 0.0))
    block = jnp.concatenate([low_rank, residue * back, rest], axis=1).astype(BF16)
    for c in range(COLS):
        out_ref[c] = block


def part_kernel(got_ref, x_ref, left_ref, right_ref, weight_ref, bias_ref, out_ref):
    last = slice(WIDE - BLOCK, WIDE)
    low_rank = got_ref[:, :, :RANK].reshape(HOST, RANK)
    grad_rank = got_ref[:, :, RANK : 2 * RANK].reshape(HOST, RANK)
    rest = got_ref[:, :, 2 * RANK :].astype(F32).reshape(HOST, BLOCK)
    residue = rest[:, 0:1] + rest[:, 1:2]
    expanded = dot(low_rank, right_ref[:, last], NN) + bias_ref[:, last]
    grad = residue * weight_ref[:, last] * (expanded + 1.0) + dot(grad_rank, left_ref[last, :], NT)
    grad = grad[:, SLICE:].astype(BF16).astype(F32)
    blank = jnp.zeros((BATCH, SLICE), F32)
    for c in range(COLS):
        k = (c % 4) * 16
        own = jnp.concatenate([grad[c * BATCH : (c + 1) * BATCH], blank], axis=1)
        bag = jnp.concatenate(
            [grad[i * BATCH : (i + 1) * BATCH, k : k + 16] for i in range(COLS)], axis=1
        )
        out_ref[c] = jnp.concatenate([own, bag], axis=0).astype(BF16)


def grads_kernel(
    place_ref,
    got_ref,
    part_ref,
    meta_ref,
    x_ref,
    counts_ref,
    left_ref,
    right_ref,
    weight_ref,
    bias_ref,
    out_ref,
    sample_ref,
    right_scr,
):
    odd = place_ref[0]
    low_rank = got_ref[:, :, :RANK].reshape(HOST, RANK)
    grad_rank = got_ref[:, :, RANK : 2 * RANK].reshape(HOST, RANK)
    rest = got_ref[:, :, 2 * RANK :].astype(F32).reshape(HOST, BLOCK)
    residue = rest[:, 0:1] + rest[:, 1:2]

    def at(r):
        z, y = r // SIDE, r % SIDE
        return jnp.where(odd == 1, z, y), jnp.where(odd == 1, y, z)

    biases, tops = [], []
    for n in range(4):
        cols = slice(n * 256, (n + 1) * 256)
        x = x_ref[:, cols]
        wide = x.astype(F32)
        expanded = dot(low_rank, right_ref[:, cols], NN) + bias_ref[:, cols]
        tops.append(jnp.sum(residue * (wide * expanded + wide), axis=0, keepdims=True))
        grad_crossed = residue * weight_ref[:, cols]
        grad_expanded = grad_crossed * wide
        biases.append(jnp.sum(grad_expanded, axis=0, keepdims=True))
        right_scr[:, cols] = dot(low_rank, grad_expanded.astype(BF16), TN)
        left = dot(x, grad_rank, TN).astype(BF16)
        grad = grad_crossed * (expanded + 1.0) + dot(grad_rank, left_ref[cols, :], NT)
        grad = grad.astype(BF16)
        for i in range(16):
            a, b = at(16 * n + i)
            out_ref[a, b, :, :RANK] = left[16 * i : 16 * i + 16]
        for i in range(4):
            t = 4 * n + i
            if t < TABLES:
                medium = dot(grad[:, i * SLICE : (i + 1) * SLICE], counts_ref[t], TN).astype(BF16)
            else:
                medium = jnp.zeros((SLICE, NAMES), BF16)
            for k in range(4):
                a, b = at(4 * t + k)
                out_ref[a, b, :, 2 * RANK : 2 * RANK + NAMES] = medium[16 * k : 16 * k + 16]
    for r in range(ROWS):
        a, b = at(r)
        band = right_scr[8 * r : 8 * r + 8, :]
        out_ref[a, b, :, RANK : 2 * RANK] = jnp.concatenate(
            [band[:, :RANK], band[:, RANK:]], axis=0
        ).astype(BF16)

    bags = [
        jnp.concatenate(
            [meta_ref[c, BATCH : BATCH + 16, :].astype(F32)[i : i + 1] for i in range(4)], axis=1
        )
        for c in range(COLS)
    ]
    bag = subs((BATCH, ROWS * CAP)).astype(F32)
    hot = jnp.concatenate([jnp.where(b == bag, 1.0, 0.0) for b in bags], axis=0).astype(BF16)
    own = jnp.where(
        place_ref[1] == 1,
        part_ref[1, BATCH:, :].astype(F32),
        part_ref[0, BATCH:, :].astype(F32),
    )
    spread = jnp.concatenate([own] * COLS, axis=0)
    spread = jnp.where(
        subs((HOST, BLOCK)) // BATCH == lanes((HOST, BLOCK)) // 16, spread, 0.0
    ).astype(BF16)
    back = dot(hot, spread, TN).reshape(ROWS, CAP, BLOCK)
    back = jnp.concatenate([back[:, :, :SLICE], back[:, :, SLICE:]], axis=1)

    bias = jnp.concatenate(biases, axis=1)
    top = jnp.concatenate(tops, axis=1)
    blank = jnp.zeros((12, SLICE), F32)
    vectors = []
    for b in range(SIDE):
        pieces = [
            v[:, b * BLOCK + h * SLICE : b * BLOCK + (h + 1) * SLICE]
            for v in (bias, top)
            for h in range(2)
        ]
        vectors.append(jnp.concatenate(pieces + [blank], axis=0))
    vectors = jnp.stack(vectors, axis=0)
    out_ref[:, :, :, 2 * RANK + NAMES : 2 * RANK + NAMES + SLICE] = jnp.broadcast_to(
        vectors[None], (SIDE, SIDE, 16, SLICE)
    ).astype(BF16)
    low = back.astype(BF16)
    for r in range(ROWS):
        a, b = at(r)
        out_ref[a, b, :, 2 * RANK + NAMES + SLICE :] = low[r]
    sample_ref[...] = jnp.concatenate(
        [part_ref[c, :BATCH, :SLICE].astype(F32) for c in range(COLS)], axis=1
    ).astype(BF16)


SUMS = 2 * RANK + NAMES


def middle_kernel(got_ref, out_ref):
    vectors = []
    for b in range(SIDE):
        total = got_ref[0, b].astype(F32)
        for a in range(1, SIDE):
            total += got_ref[a, b].astype(F32)
        out_ref[b, :, :SUMS] = total[:, :SUMS].astype(BF16)
        vectors.append(total[:4, SUMS : SUMS + SLICE])
        for a in range(0, SIDE, 2):
            pair = [got_ref[a + i, b, :, SUMS + SLICE :].astype(F32) for i in range(2)]
            at = SUMS + a * SLICE
            out_ref[b, :, at : at + BLOCK] = jnp.concatenate(pair, axis=1).astype(BF16)
    packed = jnp.concatenate(
        [jnp.concatenate(vectors[:4], axis=0), jnp.concatenate(vectors[4:], axis=0)], axis=1
    ).astype(BF16)
    for b in range(SIDE):
        out_ref[b, :, SUMS + 512 :] = packed


def last_kernel(
    place_ref,
    got_ref,
    meta_ref,
    left_ref,
    right_ref,
    bias_ref,
    top_ref,
    giant_ref,
    medium_ref,
    data_scr,
):
    odd = place_ref[0]
    sums = got_ref[0, :, :SUMS].astype(F32)
    packed = got_ref[0, :, SUMS + 512 :].astype(F32)
    for a in range(1, SIDE):
        sums += got_ref[a, :, :SUMS].astype(F32)
        packed += got_ref[a, :, SUMS + 512 :].astype(F32)
    left_ref[...] = sums[:, :RANK]
    right = sums[:, RANK : 2 * RANK]
    right_ref[...] = jnp.concatenate([right[:8], right[8:]], axis=1)
    medium = sums[:, 2 * RANK :].astype(BF16)
    for r in range(ROWS):
        medium_ref[r] = medium
    for v, ref in ((0, bias_ref), (2, top_ref)):
        pieces = []
        for b in range(SIDE):
            at = (b // 4) * SLICE
            for h in range(2):
                i = 4 * (b % 4) + v + h
                pieces.append(packed[i : i + 1, at : at + SLICE])
        ref[...] = jnp.concatenate(pieces, axis=1)

    for second in range(SIDE):
        for first in range(SIDE):
            at = SUMS + first * SLICE
            block = got_ref[second, :, at : at + SLICE].astype(F32)
            r = jnp.where(odd == 1, first * SIDE + second, second * SIDE + first)
            data_scr[r] = jnp.concatenate([block[:CAP], block[CAP:]], axis=1)
    data = data_scr[...].reshape(ROWS * CAP, BLOCK)
    group = lanes((ROWS * CAP, BLOCK)) // 16
    row = subs((1024, ROWS * CAP)).astype(F32) + 1.0
    total = jnp.zeros((1024, BLOCK), F32)
    for c in range(COLS):
        meta = meta_ref[c, BATCH : BATCH + 16, :].astype(F32)
        name = jnp.concatenate(
            [meta[4 + i : 5 + i] * 32.0 + meta[8 + i : 9 + i] for i in range(4)], axis=1
        )
        total += dot(one_hot(name == row), jnp.where(group == c, data, 0.0).astype(BF16), NN)
    for shift in (64, 32, 16):
        total = total + pltpu.roll(total, shift, 1)
    slot = lanes((BLOCK, BLOCK)) // 16
    packed = jnp.zeros((BLOCK, BLOCK), F32)
    for i in range(8):
        packed = jnp.where(slot == i, total[i * BLOCK : (i + 1) * BLOCK], packed)
    packed = packed.astype(BF16)
    for c in range(COLS):
        giant_ref[c] = packed


def giant_kernel(got_ref, out_ref):
    slot = lanes((BLOCK, BLOCK)) // 16
    for i in range(8):
        block = jnp.zeros((BLOCK, BLOCK), F32)
        for c in range(COLS):
            piece = got_ref[c].astype(F32)
            shift = ((c - i) * 16) % BLOCK
            if shift:
                piece = pltpu.roll(piece, shift, 1)
            block = jnp.where(slot == c, piece, block)
        out_ref[i * BLOCK : (i + 1) * BLOCK, :] = block


def medium_kernel(got_ref, out_ref):
    for t in range(TABLES):
        block = got_ref[4 * t : 4 * t + 4].astype(F32).reshape(SLICE, NAMES)
        out_ref[t] = block.T


def sides():
    first, second = [], []
    for c in range(COLS):
        for k in range(SIDE):
            along_y = [(k * SIDE + y) * COLS + c for y in range(SIDE)]
            along_z = [(z * SIDE + k) * COLS + c for z in range(SIDE)]
            first.append(along_z if c % 2 else along_y)
            second.append(along_y if c % 2 else along_z)
    return first, second


def swap(value, axis, groups=None):
    return lax.all_to_all(
        value, axis, split_axis=0, concat_axis=0, tiled=True, axis_index_groups=groups
    )


def body(
    giant_table,
    look_row,
    look_owner,
    look_bag,
    look_count,
    medium_tables,
    medium_ids,
    medium_lengths,
    dense_features,
    click_labels,
    cross_left,
    cross_right,
    cross_bias,
    top_weight,
):
    first, second = sides()
    col = lax.axis_index("col")
    place = jnp.stack([col % 2, col // 4]).astype(I32)
    bias, weight = cross_bias.reshape(1, WIDE), top_weight.reshape(1, WIDE)
    live = jnp.arange(4)[None, None, :] < medium_lengths[:, :, None]
    ids = jnp.where(live, medium_ids, NAMES).reshape(BATCH, 4 * TABLES).astype(BF16)
    ids = jnp.pad(ids, ((0, 0), (0, SLICE - 4 * TABLES)))

    send, names = call(
        route_kernel,
        (struct((ROWS, 2 * CAP, BLOCK), BF16), struct((8, BLOCK), F32)),
        look_count,
        look_row.reshape(1, SLOTS),
        look_owner,
        look_bag.reshape(1, SLOTS),
        giant_table,
        smem=(0,),
    )
    got = swap(send, "row")
    send = call(
        pool_kernel, struct((COLS, 48, BLOCK), BF16), got, dense_features, ids, names
    )
    meta = swap(send, "col")
    send, x, counts = call(
        cross_kernel,
        (
            struct((COLS, BATCH, 2 * RANK + BLOCK), BF16),
            struct((HOST, WIDE), BF16),
            struct((TABLES, HOST, NAMES), BF16),
        ),
        meta,
        medium_tables,
        cross_left,
        cross_right,
        weight,
        bias,
    )
    got = swap(send, "col")
    send = call(
        residue_kernel,
        struct((COLS, BATCH, 2 * RANK + BLOCK), BF16),
        got,
        click_labels.reshape(BATCH, 1),
    )
    ranks = swap(send, "col")
    send = call(
        part_kernel,
        struct((COLS, 2 * BATCH, BLOCK), BF16),
        ranks,
        x,
        cross_left,
        cross_right,
        weight,
        bias,
    )
    parts = swap(send, "col")
    send, sample_grads = call(
        grads_kernel,
        (
            struct((SIDE, SIDE, 16, SUMS + BLOCK), BF16),
            struct((BATCH, COLS * SLICE), BF16),
        ),
        place,
        ranks,
        parts,
        meta,
        x,
        counts,
        cross_left,
        cross_right,
        weight,
        bias,
        smem=(0,),
        scratch=(pltpu.VMEM((RANK, WIDE), F32),),
    )
    got = swap(send, ("row", "col"), first)
    send = call(middle_kernel, struct((SIDE, 16, SUMS + 512 + BLOCK), BF16), got)
    got = swap(send, ("row", "col"), second)
    left_grad, right_grad, bias_grad, top_grad, giant, medium = call(
        last_kernel,
        (
            struct((16, RANK), F32),
            struct((8, WIDE), F32),
            struct((1, WIDE), F32),
            struct((1, WIDE), F32),
            struct((COLS, BLOCK, BLOCK), BF16),
            struct((ROWS, 16, NAMES), BF16),
        ),
        place,
        got,
        meta,
        smem=(0,),
        scratch=(pltpu.VMEM((ROWS, CAP, BLOCK), F32),),
    )
    giant_grad = call(giant_kernel, struct((1024, BLOCK), F32), swap(giant, "col"))
    medium_grad = call(
        medium_kernel, struct((TABLES, NAMES, SLICE), F32), swap(medium, "row")
    )
    return (
        sample_grads,
        giant_grad,
        medium_grad,
        left_grad,
        right_grad,
        bias_grad.reshape(WIDE),
        top_grad.reshape(WIDE),
    )


def solution(mesh):
    both = P(("row", "col"))
    placed = (
        P("row", None),
        both,
        P(("row", "col"), None),
        both,
        both,
        P(None, None, "col"),
        P(("row", "col"), None, None),
        P(("row", "col"), None),
        P(("row", "col"), None),
        both,
        P("col", None),
        P(None, "col"),
        P("col"),
        P("col"),
    )
    return jax.shard_map(
        body,
        mesh=mesh,
        in_specs=placed,
        out_specs=(
            P(("row", "col"), None),
            P("row", None),
            P(None, None, "col"),
            P(("col", "row"), None),
            P("row", "col"),
            P("col"),
            P("col"),
        ),
        check_vma=False,
    )
```

time: 913 us -> 199 us (0.22)
  waiting for transfers between devices: 352 us -> 46.4 us
  other arithmetic: 134 us -> 0.84 us
  local copies, waits for them, and re-layouts: 141 us -> 10.9 us
  blocking collectives: 193 us -> 81.1 us
  Pallas kernels: 0 us -> 18 us
  starting transfers between devices: 54.9 us -> 37.7 us
  between operations: 16.9 us -> 1.55 us
  matrix products: 11.5 us -> 0 us
    reduce_scatter x1 -> x0, waiting for transfers between devices: 241 us -> none  [body(): lax.psum_scatter(lax.dot_general(columns, grad_rank, (((0,), (0,)), ((),...]
    psum x3 -> x0, blocking collectives: 158 us -> none  [the longest x1 115 us: body(): lax.psum((local_medium, local_bias, local_top), 'row')]
    psum x3 -> x0, waiting for transfers between devices: 96.8 us -> none  [the longest x1 57.5 us: body(): lax.psum(lax.dot_general(grad_expanded_low, cross_right, (((1,), (1,)), (...]
    unnamed x4 -> x0, other arithmetic: 83.6 us -> none
    all_to_all x0 -> x4, blocking collectives: none -> 81.1 us  [swap(): lax.all_to_all(value, axis, split_axis=0, concat_axis=0, tiled=True, axis...]
    gather x16 -> x0, local copies, waits for them, and re-layouts: 60.6 us -> none  [the longest x15 58.7 us: body(): medium_tables[table_index][host_ids[:, table_index, :]]]
    unnamed x92 -> x31, local copies, waits for them, and re-layouts: 51.9 us -> 10.7 us
    all_to_all x5, waiting for transfers between devices: 14.5 us -> 46.4 us  [swap(): lax.all_to_all(value, axis, split_axis=0, concat_axis=0, tiled=True, axis...]
  transfers between devices with their start and end apart: 9 -> 5, of which waited for: 6 -> 5; matrix products, arithmetic and copies ran while one was open for 28% -> 1% of each run, Pallas kernels for 0% -> 1%
where the time goes in v1:
time: 199 us; the launch traced here: 196 us
  blocking collectives  81.1 us (41%)
  waiting for transfers between devices  46.4 us (23%)
  starting transfers between devices  37.7 us (19%)
  Pallas kernels  18 us (9%)
  local copies, waits for them, and re-layouts  10.9 us (5%)
    all_to_all x4, blocking collectives, swap(): lax.all_to_all(value, axis, split_axis=0, concat_axis=0, tiled=True, axis...  81.1 us
    all_to_all x5, waiting for transfers between devices, swap(): lax.all_to_all(value, axis, split_axis=0, concat_axis=0, tiled=True, axis...  46.4 us
    all_to_all x5, starting transfers between devices, swap(): lax.all_to_all(value, axis, split_axis=0, concat_axis=0, tiled=True, axis...  37.7 us
    pallas_call x10, Pallas kernels, call(): pl.pallas_call(kernel, out_shape=outs, in_specs=[pl.BlockSpec(memory_spac...  18 us
    unnamed x31, local copies, waits for them, and re-layouts  10.7 us
  transfers between devices with their start and end apart: 5, of which 5 were waited for; matrix products, arithmetic and copies ran while one was open for 1% of the time, Pallas kernels for 1%

profile of v1, /device:TPU:1, one launch (start us, length us, event | category | flops | bytes accessed | tf_op | source)
XLA Modules:
  0.0 196.4 jit_solution(911907009088031469)
XLA Ops:
  0.6 0.0 copy-start.1
  0.6 0.0 copy-start
  1.4 0.8 copy.26.owner_ref
  2.3 0.0 copy-start.7
  2.3 0.9 copy-done.7
  3.2 0.7 copy-done.11
  3.9 0.7 copy-done.12
  4.6 1.5 shard_map.189
  6.0 17.1 %all-to-all-start = ((bf16[64,16,128]{2,1,0:T(8,128)(2,1)}), bf16[64,16,128]{2,1,0:T(8,128)(2,1)S(1)}, u32[]{:S(2)}, u32[]{:S(2)}) async-start(bf16[64,16,128]{2,1,0:T(8,128)(2,1)} %get-tuple-element.20), calls=%async_computation | async-start | bytes 524288 | tf_op jit(solution)/shard_map/all_to_all | solution.py:403
  23.2 0.8 select_convert_fusion
  24.0 0.1 copy.27
  24.1 11.8 %all-to-all-done.got_ref = bf16[64,16,128]{2,1,0:T(8,128)(2,1)S(1)} async-done(((bf16[64,16,128]{2,1,0:T(8,128)(2,1)}), bf16[64,16,128]{2,1,0:T(8,128)(2,1)S(1)}, u32[]{:S(2)}, u32[]{:S(2)}) %all-to-all-start) | async-done | bytes 262176 | tf_op jit(solution)/shard_map/all_to_all | solution.py:403
  35.8 0.7 copy-done.10
  36.6 0.9 shard_map.190
  37.5 7.5 %all-to-all-start.1 = ((bf16[8,48,128]{2,1,0:T(8,128)(2,1)}), bf16[8,48,128]{2,1,0:T(8,128)(2,1)S(1)}, u32[]{:S(2)}, u32[]{:S(2)}) async-start(bf16[8,48,128]{2,1,0:T(8,128)(2,1)} %shard_map.190), calls=%async_computation.1 | async-start | bytes 196608 | tf_op jit(solution)/shard_map/all_to_all | solution.py:403
  45.0 1.5 copy.28.tables_ref
  46.5 3.5 %all-to-all-done.1.got_ref.meta_ref = bf16[8,48,128]{2,1,0:T(8,128)(2,1)S(1)} async-done(((bf16[8,48,128]{2,1,0:T(8,128)(2,1)}), bf16[8,48,128]{2,1,0:T(8,128)(2,1)S(1)}, u32[]{:S(2)}, u32[]{:S(2)}) %all-to-all-start.1) | async-done | bytes 98336 | tf_op jit(solution)/shard_map/all_to_all | solution.py:403
  50.0 0.0 copy-done.1
  50.0 0.0 copy-done
  50.0 0.0 copy-done.8
  50.0 0.0 copy-done.9
  50.0 4.4 %shard_map.191 = (bf16[8,32,1152]{2,1,0:T(8,128)(2,1)S(1)}, bf16[256,1024]{1,0:T(8,128)(2,1)S(1)}, bf16[15,256,256]{2,1,0:T(8,128)(2,1)}) custom-call(bf16[8,48,128]{2,1,0:T(8,128)(2,1)S(1)} %all-to-all-done.1.got_ref.meta_ref, bf16[15,256,64]{2,1,0:T(8,128)(2,1)S(1)} %copy.28.tables_ref, bf16[1024,512]{1,0:T(8,128)(2,1)S(1)} %copy-done, ...), custom_call_target="tpu_custom_call" | custom-call | tf_op jit(solution)/shard_map/pallas_call | solution.py:42
  54.4 0.8 copy-done.2
  55.2 0.8 copy-done.5
  56.0 4.4 %all-to-all-start.2 = ((bf16[8,32,1152]{2,1,0:T(8,128)(2,1)}), bf16[8,32,1152]{2,1,0:T(8,128)(2,1)S(1)}, u32[]{:S(2)}, u32[]{:S(2)}) async-start(bf16[8,32,1152]{2,1,0:T(8,128)(2,1)} %copy-done.5), calls=%async_computation.2 | async-start | bytes 1179648 | tf_op jit(solution)/shard_map/all_to_all | solution.py:403
  60.4 0.0 copy-done.13
  60.4 0.1 copy.29.label_ref
  60.5 10.1 %all-to-all-done.2.got_ref = bf16[8,32,1152]{2,1,0:T(8,128)(2,1)S(1)} async-done(((bf16[8,32,1152]{2,1,0:T(8,128)(2,1)}), bf16[8,32,1152]{2,1,0:T(8,128)(2,1)S(1)}, u32[]{:S(2)}, u32[]{:S(2)}) %all-to-all-start.2) | async-done | bytes 589856 | tf_op jit(solution)/shard_map/all_to_all | solution.py:403
  70.6 0.3 shard_map.192
  70.9 13.6 %all_to_all.45.got_ref = bf16[8,32,1152]{2,1,0:T(8,128)(2,1)S(1)} all-to-all(bf16[8,32,1152]{2,1,0:T(8,128)(2,1)S(1)} %shard_map.192), channel_id=1, replica_groups=mesh['row'=64,'col'=8] {'col'}, dimensions={0} | all-to-all | bytes 1179648 | tf_op jit(solution)/shard_map/all_to_all | solution.py:403
  84.5 0.4 shard_map.193
  84.9 0.0 copy-start.6
  84.9 0.6 copy-done.6
  85.5 4.0 %all-to-all-start.4 = ((bf16[8,64,128]{2,1,0:T(8,128)(2,1)}), bf16[8,64,128]{2,1,0:T(8,128)(2,1)S(1)}, u32[]{:S(2)}, u32[]{:S(2)}) async-start(bf16[8,64,128]{2,1,0:T(8,128)(2,1)} %copy-done.6), calls=%async_computation.4 | async-start | bytes 262144 | tf_op jit(solution)/shard_map/all_to_all | solution.py:403
  89.6 0.1 pad_add_fusion.place_ref
  89.6 5.2 %all-to-all-done.4.part_ref = bf16[8,64,128]{2,1,0:T(8,128)(2,1)S(1)} async-done(((bf16[8,64,128]{2,1,0:T(8,128)(2,1)}), bf16[8,64,128]{2,1,0:T(8,128)(2,1)S(1)}, u32[]{:S(2)}, u32[]{:S(2)}) %all-to-all-start.4) | async-done | bytes 131104 | tf_op jit(solution)/shard_map/all_to_all | solution.py:403
  94.9 1.5 copy-done.4
  96.4 4.4 %shard_map.194 = (bf16[8,8,16,1408]{3,2,1,0:T(8,128)(2,1)}, bf16[32,512]{1,0:T(8,128)(2,1)}) custom-call(s32[2]{0:T(128)S(1)} %pad_add_fusion.place_ref, bf16[8,32,1152]{2,1,0:T(8,128)(2,1)S(1)} %all_to_all.45.got_ref, bf16[8,64,128]{2,1,0:T(8,128)(2,1)S(1)} %all-to-all-done.4.part_ref, bf16[8,48,128]{2,1,0:T(8,128)(2,1)S(1)} %all-to-all-done.1.got_ref.meta_ref, ...), custom_call_target="tpu_custom_call" | custom-call | tf_op jit(solution)/shard_map/pallas_call | solution.py:42
  100.8 41.0 %all_to_all.46.got_ref = bf16[8,8,16,1408]{3,2,1,0:T(8,128)(2,1)S(1)} all-to-all(bf16[8,8,16,1408]{3,2,1,0:T(8,128)(2,1)} %get-tuple-element.26), channel_id=1, replica_groups={{0,8,16,24,32,40,48,56},{64,72,80,88,96,104,112,120},{128,136,144,152,1..., dimensions={0} | all-to-all | bytes 5767168 | tf_op jit(solution)/shard_map/all_to_all | solution.py:403
  141.8 0.4 shard_map.195
  142.2 14.4 %all_to_all.47.got_ref = bf16[8,16,1920]{2,1,0:T(8,128)(2,1)S(1)} all-to-all(bf16[8,16,1920]{2,1,0:T(8,128)(2,1)S(1)} %shard_map.195), channel_id=1, replica_groups={{0,64,128,192,256,320,384,448},{8,72,136,200,264,328,392,456},{16,80,14..., dimensions={0} | all-to-all | bytes 983040 | tf_op jit(solution)/shard_map/all_to_all | solution.py:403
  156.6 4.1 %shard_map.196 = (f32[16,512]{1,0:T(8,128)}, f32[8,1024]{1,0:T(8,128)}, f32[1,1024]{1,0:T(1,128)}, f32[1,1024]{1,0:T(1,128)}, bf16[8,128,128]{2,1,0:T(8,128)(2,1)S(1)}, /*index=5*/bf16[64,16,256]{2,1,0:T(8,128)(2,1)}) custom-call(s32[2]{0:T(128)S(1)} %pad_add_fusion.place_ref, bf16[8,16,1920]{2,1,0:T(8,128)(2,1)S(1)} %all_to_all.47.got_ref, ...), custom_call_target="tpu_custom_call" | custom-call | tf_op jit(solution)/shard_map/pallas_call | solution.py:42
  160.7 12.1 %all_to_all.48.got_ref = bf16[8,128,128]{2,1,0:T(8,128)(2,1)S(1)} all-to-all(bf16[8,128,128]{2,1,0:T(8,128)(2,1)S(1)} %get-tuple-element.27), channel_id=1, replica_groups=mesh['row'=64,'col'=8] {'col'}, dimensions={0} | all-to-all | bytes 524288 | tf_op jit(solution)/shard_map/all_to_all | solution.py:403
  172.8 4.6 %all-to-all-start.8 = ((bf16[64,16,256]{2,1,0:T(8,128)(2,1)}), bf16[64,16,256]{2,1,0:T(8,128)(2,1)S(1)}, u32[]{:S(2)}, u32[]{:S(2)}) async-start(bf16[64,16,256]{2,1,0:T(8,128)(2,1)} %get-tuple-element.28), calls=%async_computation.8 | async-start | bytes 1048576 | tf_op jit(solution)/shard_map/all_to_all | solution.py:403
  177.4 1.3 shard_map.197
  178.7 15.8 %all-to-all-done.8.got_ref = bf16[64,16,256]{2,1,0:T(8,128)(2,1)S(1)} async-done(((bf16[64,16,256]{2,1,0:T(8,128)(2,1)}), bf16[64,16,256]{2,1,0:T(8,128)(2,1)S(1)}, u32[]{:S(2)}, u32[]{:S(2)}) %all-to-all-start.8) | async-done | bytes 524320 | tf_op jit(solution)/shard_map/all_to_all | solution.py:403
  194.6 0.3 shard_map.198
  194.9 1.5 copy.30
  (13 shorter events, 0.0 us)
Async XLA Ops:
  0.6 49.4 %copy-start.1 = (bf16[512,1024]{1,0:T(8,128)(2,1)S(1)}, bf16[512,1024]{1,0:T(8,128)(2,1)}, u32[]{:S(2)}) copy-start(bf16[512,1024]{1,0:T(8,128)(2,1)} %right_ref.5) | copy-start | bytes 3145732
  0.6 49.4 %copy-start = (bf16[1024,512]{1,0:T(8,128)(2,1)S(1)}, bf16[1024,512]{1,0:T(8,128)(2,1)}, u32[]{:S(2)}) copy-start(bf16[1024,512]{1,0:T(8,128)(2,1)} %left_ref.5) | copy-start | bytes 3145732
  2.3 1.0 copy-start.7
  3.2 0.7 copy-start.11
  3.9 0.7 copy-start.12
  4.6 45.4 %copy-start.8 = (f32[1024]{0:T(1024)S(1)}, f32[1024]{0:T(1024)}, u32[]{:S(2)}) copy-start(f32[1024]{0:T(1024)} %param.27) | copy-start | bytes 12292
  4.6 45.4 %copy-start.9 = (f32[1024]{0:T(1024)S(1)}, f32[1024]{0:T(1024)}, u32[]{:S(2)}) copy-start(f32[1024]{0:T(1024)} %param.26) | copy-start | bytes 12292
  6.0 29.8 %all-to-all-start = ((bf16[64,16,128]{2,1,0:T(8,128)(2,1)}), bf16[64,16,128]{2,1,0:T(8,128)(2,1)S(1)}, u32[]{:S(2)}, u32[]{:S(2)}) async-start(bf16[64,16,128]{2,1,0:T(8,128)(2,1)} %get-tuple-element.20), calls=%async_computation | async-start | bytes 524288 | tf_op jit(solution)/shard_map/all_to_all | solution.py:403
  35.8 0.7 copy-start.10
  37.5 12.5 %all-to-all-start.1 = ((bf16[8,48,128]{2,1,0:T(8,128)(2,1)}), bf16[8,48,128]{2,1,0:T(8,128)(2,1)S(1)}, u32[]{:S(2)}, u32[]{:S(2)}) async-start(bf16[8,48,128]{2,1,0:T(8,128)(2,1)} %shard_map.190), calls=%async_computation.1 | async-start | bytes 196608 | tf_op jit(solution)/shard_map/all_to_all | solution.py:403
  45.0 15.4 %copy-start.13 = (s32[32]{0:T(128)S(1)}, s32[32]{0:T(128)}, u32[]{:S(2)}) copy-start(s32[32]{0:T(128)} %param.23) | copy-start | bytes 388
  54.4 0.8 copy-start.2
  55.2 0.8 copy-start.5
  56.0 28.5 %copy-start.3 = (bf16[256,1024]{1,0:T(8,128)(2,1)S(1)}, bf16[256,1024]{1,0:T(8,128)(2,1)}, u32[]{:S(2)}) copy-start(bf16[256,1024]{1,0:T(8,128)(2,1)} %copy-done.2) | copy-start | bytes 1572868
  56.0 14.6 %all-to-all-start.2 = ((bf16[8,32,1152]{2,1,0:T(8,128)(2,1)}), bf16[8,32,1152]{2,1,0:T(8,128)(2,1)S(1)}, u32[]{:S(2)}, u32[]{:S(2)}) async-start(bf16[8,32,1152]{2,1,0:T(8,128)(2,1)} %copy-done.5), calls=%async_computation.2 | async-start | bytes 1179648 | tf_op jit(solution)/shard_map/all_to_all | solution.py:403
  84.9 0.7 copy-start.6
  85.5 9.3 %all-to-all-start.4 = ((bf16[8,64,128]{2,1,0:T(8,128)(2,1)}), bf16[8,64,128]{2,1,0:T(8,128)(2,1)S(1)}, u32[]{:S(2)}, u32[]{:S(2)}) async-start(bf16[8,64,128]{2,1,0:T(8,128)(2,1)} %copy-done.6), calls=%async_computation.4 | async-start | bytes 262144 | tf_op jit(solution)/shard_map/all_to_all | solution.py:403
  94.9 1.5 copy-start.4
  172.8 21.8 %all-to-all-start.8 = ((bf16[64,16,256]{2,1,0:T(8,128)(2,1)}), bf16[64,16,256]{2,1,0:T(8,128)(2,1)S(1)}, u32[]{:S(2)}, u32[]{:S(2)}) async-start(bf16[64,16,256]{2,1,0:T(8,128)(2,1)} %get-tuple-element.28), calls=%async_computation.8 | async-start | bytes 1048576 | tf_op jit(solution)/shard_map/all_to_all | solution.py:403

commit v2 on v1

--- a/solution.py
+++ b/solution.py
@@ -38,7 +38,7 @@
     return jnp.where(mask, 1.0, 0.0).astype(BF16)
 
 
-def call(kernel, outs, *args, smem=(), scratch=()):
+def call(kernel, outs, *args, smem=(), scratch=(), vmem=16):
     return pl.pallas_call(
         kernel,
         out_shape=outs,
@@ -48,7 +48,7 @@
         ],
         out_specs=jax.tree.map(lambda _: pl.BlockSpec(memory_space=pltpu.VMEM), outs),
         scratch_shapes=list(scratch),
-        compiler_params=pltpu.CompilerParams(vmem_limit_bytes=48 * 2**20),
+        compiler_params=pltpu.CompilerParams(vmem_limit_bytes=vmem * 2**20),
     )(*args)
 
 
@@ -63,14 +63,14 @@
         return jnp.sum(jnp.where(eye, ref[...].astype(F32), 0.0), axis=1, keepdims=True)
 
     row, bag = column(row_ref), column(bag_ref)
-    owner = owner_ref[...]
+    owner = column(owner_ref)
     live = subs((SLOTS, BLOCK)) < count_ref[0]
-    hits = jnp.where((owner == lanes((SLOTS, BLOCK))) & live, 1.0, 0.0)
+    hits = jnp.where((owner == lanes((SLOTS, BLOCK)).astype(F32)) & live, 1.0, 0.0)
     before = one_hot(subs((SLOTS, SLOTS)) > lanes((SLOTS, SLOTS)))
     earlier = dot(before, hits.astype(BF16), NN)
     place = jnp.sum(earlier * hits, axis=1, keepdims=True)
     alive = jnp.sum(hits, axis=1, keepdims=True)
-    target = jnp.where(alive > 0.5, owner.astype(F32) * CAP + place, -1.0)
+    target = jnp.where(alive > 0.5, owner * CAP + place, -1.0)
     at = target == lanes((SLOTS, ROWS * CAP)).astype(F32)
     looked = dot(one_hot(row == lanes((SLOTS, 1024)).astype(F32)), table_ref[...], NN)
     both = jnp.concatenate(
@@ -124,7 +124,7 @@
             count += jnp.where(ids[:, 4 * t + j : 4 * t + j + 1] == name, 1.0, 0.0)
         low = count.astype(BF16)
         counts_ref[t] = low
-        pieces.append(dot(low, tables_ref[t], NN))
+        pieces.append(dot(low, tables_ref[t], NT))
         if t % 2:
             x_ref[:, (t // 2) * BLOCK : (t // 2 + 1) * BLOCK] = jnp.concatenate(
                 pieces, axis=1
@@ -309,30 +309,18 @@
         out_ref[b, :, SUMS + 512 :] = packed
 
 
-def last_kernel(
-    place_ref,
-    got_ref,
-    meta_ref,
-    left_ref,
-    right_ref,
-    bias_ref,
-    top_ref,
-    giant_ref,
-    medium_ref,
-    data_scr,
-):
-    odd = place_ref[0]
+def last_kernel(got_ref, left_ref, right_ref, bias_ref, top_ref, medium_ref):
     sums = got_ref[0, :, :SUMS].astype(F32)
     packed = got_ref[0, :, SUMS + 512 :].astype(F32)
     for a in range(1, SIDE):
         sums += got_ref[a, :, :SUMS].astype(F32)
         packed += got_ref[a, :, SUMS + 512 :].astype(F32)
+    medium = sums[:, 2 * RANK :].astype(BF16)
+    for r in range(ROWS):
+        medium_ref[r] = medium
     left_ref[...] = sums[:, :RANK]
     right = sums[:, RANK : 2 * RANK]
     right_ref[...] = jnp.concatenate([right[:8], right[8:]], axis=1)
-    medium = sums[:, 2 * RANK :].astype(BF16)
-    for r in range(ROWS):
-        medium_ref[r] = medium
     for v, ref in ((0, bias_ref), (2, top_ref)):
         pieces = []
         for b in range(SIDE):
@@ -342,6 +330,9 @@
                 pieces.append(packed[i : i + 1, at : at + SLICE])
         ref[...] = jnp.concatenate(pieces, axis=1)
 
+
+def rows_kernel(place_ref, got_ref, meta_ref, out_ref, data_scr):
+    odd = place_ref[0]
     for second in range(SIDE):
         for first in range(SIDE):
             at = SUMS + first * SLICE
@@ -364,9 +355,7 @@
     packed = jnp.zeros((BLOCK, BLOCK), F32)
     for i in range(8):
         packed = jnp.where(slot == i, total[i * BLOCK : (i + 1) * BLOCK], packed)
-    packed = packed.astype(BF16)
-    for c in range(COLS):
-        giant_ref[c] = packed
+    out_ref[0] = packed.astype(BF16)
 
 
 def giant_kernel(got_ref, out_ref):
@@ -385,7 +374,7 @@
 def medium_kernel(got_ref, out_ref):
     for t in range(TABLES):
         block = got_ref[4 * t : 4 * t + 4].astype(F32).reshape(SLICE, NAMES)
-        out_ref[t] = block.T
+        out_ref[t] = block
 
 
 def sides():
@@ -434,10 +423,11 @@
         (struct((ROWS, 2 * CAP, BLOCK), BF16), struct((8, BLOCK), F32)),
         look_count,
         look_row.reshape(1, SLOTS),
-        look_owner,
+        look_owner.reshape(1, SLOTS),
         look_bag.reshape(1, SLOTS),
         giant_table,
         smem=(0,),
+        vmem=60,
     )
     got = swap(send, "row")
     send = call(
@@ -452,7 +442,7 @@
             struct((TABLES, HOST, NAMES), BF16),
         ),
         meta,
-        medium_tables,
+        jnp.swapaxes(medium_tables, 1, 2),
         cross_left,
         cross_right,
         weight,
@@ -495,29 +485,39 @@
         bias,
         smem=(0,),
         scratch=(pltpu.VMEM((RANK, WIDE), F32),),
+        vmem=24,
     )
     got = swap(send, ("row", "col"), first)
     send = call(middle_kernel, struct((SIDE, 16, SUMS + 512 + BLOCK), BF16), got)
     got = swap(send, ("row", "col"), second)
-    left_grad, right_grad, bias_grad, top_grad, giant, medium = call(
+    left_grad, right_grad, bias_grad, top_grad, medium = call(
         last_kernel,
         (
             struct((16, RANK), F32),
             struct((8, WIDE), F32),
             struct((1, WIDE), F32),
             struct((1, WIDE), F32),
-            struct((COLS, BLOCK, BLOCK), BF16),
             struct((ROWS, 16, NAMES), BF16),
         ),
+        got,
+    )
+    medium = swap(medium, "row")
+    giant = call(
+        rows_kernel,
+        struct((1, BLOCK, BLOCK), BF16),
         place,
         got,
         meta,
         smem=(0,),
         scratch=(pltpu.VMEM((ROWS, CAP, BLOCK), F32),),
     )
-    giant_grad = call(giant_kernel, struct((1024, BLOCK), F32), swap(giant, "col"))
-    medium_grad = call(
-        medium_kernel, struct((TABLES, NAMES, SLICE), F32), swap(medium, "row")
+    giant_grad = call(
+        giant_kernel,
+        struct((1024, BLOCK), F32),
+        lax.all_gather(giant, "col", axis=0, tiled=True),
+    )
+    medium_grad = jnp.swapaxes(
+        call(medium_kernel, struct((TABLES, SLICE, NAMES), F32), medium), 1, 2
     )
     return (
         sample_grads,

time: 199 us -> 185 us (0.930)
  waiting for transfers between devices: 46.4 us -> 27.1 us
  blocking collectives: 81.1 us -> 96.1 us
  starting transfers between devices: 37.7 us -> 30.2 us
    all_to_all x5 -> x4, waiting for transfers between devices: 46.4 us -> 27.1 us  [swap(): lax.all_to_all(value, axis, split_axis=0, concat_axis=0, tiled=True, axis...]
    all_gather x0 -> x1, blocking collectives: none -> 15.9 us  [body(): lax.all_gather(giant, 'col', axis=0, tiled=True)]
    all_to_all x5 -> x4, starting transfers between devices: 37.7 us -> 30.2 us  [swap(): lax.all_to_all(value, axis, split_axis=0, concat_axis=0, tiled=True, axis...]
    pallas_call x10 -> x11, Pallas kernels: 18 us -> 17.5 us  [call(): pl.pallas_call(kernel, out_shape=outs, in_specs=[pl.BlockSpec(memory_spac...]
    unnamed x31 -> x32, local copies, waits for them, and re-layouts: 10.7 us -> 10.6 us
  transfers between devices with their start and end apart: 5 -> 4, of which waited for: 5 -> 3; matrix products, arithmetic and copies ran while one was open for 1% -> 1% of each run, Pallas kernels for 1% -> 3%
where the time goes in v2:
time: 185 us; the launch traced here: 184 us
  blocking collectives  96.1 us (52%)
  starting transfers between devices  30.2 us (16%)
  waiting for transfers between devices  27.1 us (15%)
  Pallas kernels  17.5 us (9%)
  local copies, waits for them, and re-layouts  10.8 us (6%)
    all_to_all x4, blocking collectives, swap(): lax.all_to_all(value, axis, split_axis=0, concat_axis=0, tiled=True, axis...  80.2 us
    all_to_all x4, starting transfers between devices, swap(): lax.all_to_all(value, axis, split_axis=0, concat_axis=0, tiled=True, axis...  30.2 us
    all_to_all x4, waiting for transfers between devices, swap(): lax.all_to_all(value, axis, split_axis=0, concat_axis=0, tiled=True, axis...  27.1 us
    pallas_call x11, Pallas kernels, call(): pl.pallas_call(kernel, out_shape=outs, in_specs=[pl.BlockSpec(memory_spac...  17.5 us
    all_gather x1, blocking collectives, body(): lax.all_gather(giant, 'col', axis=0, tiled=True)  15.9 us
    unnamed x32, local copies, waits for them, and re-layouts  10.6 us
  transfers between devices with their start and end apart: 4, of which 3 were waited for; matrix products, arithmetic and copies ran while one was open for 1% of the time, Pallas kernels for 3%

profile of v2, /device:TPU:1, one launch (start us, length us, event | category | flops | bytes accessed | tf_op | source)
XLA Modules:
  0.0 184.0 jit_solution(13991419286040162544)
XLA Ops:
  0.6 0.0 copy-start.15
  1.3 2.5 %shard_map.189 = (bf16[64,16,128]{2,1,0:T(8,128)(2,1)}, f32[8,128]{1,0:T(8,128)}) custom-call(s32[1]{0:T(128)S(6)} %copy.27.count_ref, s32[1,256]{1,0:T(1,128)} %bitcast.22, s32[1,256]{1,0:T(1,128)} %bitcast.23, s32[1,256]{1,0:T(1,128)} %bitcast.24, bf16[1024,128]{1,0:T(8,128)(2,1)} %table_ref.1), custom_call_target="tpu_custom_call" | custom-call | tf_op jit(solution)/shard_map/pallas_call | solution.py:42
  3.8 17.1 %all-to-all-start = ((bf16[64,16,128]{2,1,0:T(8,128)(2,1)}), bf16[64,16,128]{2,1,0:T(8,128)(2,1)S(1)}, u32[]{:S(2)}, u32[]{:S(2)}) async-start(bf16[64,16,128]{2,1,0:T(8,128)(2,1)} %get-tuple-element.19), calls=%async_computation | async-start | bytes 524288 | tf_op jit(solution)/shard_map/all_to_all | solution.py:392
  20.9 0.8 select_convert_fusion
  21.7 0.1 copy.25
  21.8 11.8 %all-to-all-done.got_ref = bf16[64,16,128]{2,1,0:T(8,128)(2,1)S(1)} async-done(((bf16[64,16,128]{2,1,0:T(8,128)(2,1)}), bf16[64,16,128]{2,1,0:T(8,128)(2,1)S(1)}, u32[]{:S(2)}, u32[]{:S(2)}) %all-to-all-start) | async-done | bytes 262176 | tf_op jit(solution)/shard_map/all_to_all | solution.py:392
  33.5 0.0 copy-start.13
  33.5 0.7 copy-done.13
  34.3 0.7 copy-done.14
  35.0 0.3 shard_map.190
  35.3 12.3 %all_to_all.40.got_ref.meta_ref = bf16[8,48,128]{2,1,0:T(8,128)(2,1)S(1)} all-to-all(bf16[8,48,128]{2,1,0:T(8,128)(2,1)S(1)} %shard_map.190), channel_id=1, replica_groups=mesh['row'=64,'col'=8] {'col'}, dimensions={0} | all-to-all | bytes 196608 | tf_op jit(solution)/shard_map/all_to_all | solution.py:392
  47.5 1.2 copy-done
  48.8 1.2 copy-done.2
  50.0 1.0 copy-done.8
  51.0 0.7 copy-done.9
  51.7 0.7 copy-done.11
  52.4 3.7 %shard_map.191 = (bf16[8,32,1152]{2,1,0:T(8,128)(2,1)S(1)}, bf16[256,1024]{1,0:T(8,128)(2,1)S(1)}, bf16[15,256,256]{2,1,0:T(8,128)(2,1)S(1)}) custom-call(bf16[8,48,128]{2,1,0:T(8,128)(2,1)S(1)} %all_to_all.40.got_ref.meta_ref, bf16[15,64,256]{2,1,0:T(8,128)(2,1)S(1)} %bitcast.14, bf16[1024,512]{1,0:T(8,128)(2,1)S(1)} %copy-done, ...), custom_call_target="tpu_custom_call" | custom-call | tf_op jit(solution)/shard_map/pallas_call | solution.py:42
  56.1 0.0 copy-start.4
  56.2 1.3 copy-done.4
  57.4 0.8 copy-done.6
  58.3 4.3 %all-to-all-start.2 = ((bf16[8,32,1152]{2,1,0:T(8,128)(2,1)}), bf16[8,32,1152]{2,1,0:T(8,128)(2,1)S(1)}, u32[]{:S(2)}, u32[]{:S(2)}) async-start(bf16[8,32,1152]{2,1,0:T(8,128)(2,1)} %copy-done.6), calls=%async_computation.2 | async-start | bytes 1179648 | tf_op jit(solution)/shard_map/all_to_all | solution.py:392
  62.5 0.0 copy-done.15
  62.5 0.1 copy.26.label_ref
  62.6 10.1 %all-to-all-done.2.got_ref = bf16[8,32,1152]{2,1,0:T(8,128)(2,1)S(1)} async-done(((bf16[8,32,1152]{2,1,0:T(8,128)(2,1)}), bf16[8,32,1152]{2,1,0:T(8,128)(2,1)S(1)}, u32[]{:S(2)}, u32[]{:S(2)}) %all-to-all-start.2) | async-done | bytes 589856 | tf_op jit(solution)/shard_map/all_to_all | solution.py:392
  72.7 0.3 shard_map.192
  73.0 13.6 %all_to_all.41.got_ref = bf16[8,32,1152]{2,1,0:T(8,128)(2,1)S(1)} all-to-all(bf16[8,32,1152]{2,1,0:T(8,128)(2,1)S(1)} %shard_map.192), channel_id=1, replica_groups=mesh['row'=64,'col'=8] {'col'}, dimensions={0} | all-to-all | bytes 1179648 | tf_op jit(solution)/shard_map/all_to_all | solution.py:392
  86.6 0.0 copy-done.1
  86.6 0.0 copy-done.3
  86.6 0.0 copy-done.10
  86.6 0.0 copy-done.12
  86.6 0.4 shard_map.193
  87.0 0.0 copy-start.7
  87.0 0.6 copy-done.7
  87.7 4.0 %all-to-all-start.4 = ((bf16[8,64,128]{2,1,0:T(8,128)(2,1)}), bf16[8,64,128]{2,1,0:T(8,128)(2,1)S(1)}, u32[]{:S(2)}, u32[]{:S(2)}) async-start(bf16[8,64,128]{2,1,0:T(8,128)(2,1)} %copy-done.7), calls=%async_computation.4 | async-start | bytes 262144 | tf_op jit(solution)/shard_map/all_to_all | solution.py:392
  91.7 0.1 pad_add_fusion.place_ref
  91.8 5.2 %all-to-all-done.4.part_ref = bf16[8,64,128]{2,1,0:T(8,128)(2,1)S(1)} async-done(((bf16[8,64,128]{2,1,0:T(8,128)(2,1)}), bf16[8,64,128]{2,1,0:T(8,128)(2,1)S(1)}, u32[]{:S(2)}, u32[]{:S(2)}) %all-to-all-start.4) | async-done | bytes 131104 | tf_op jit(solution)/shard_map/all_to_all | solution.py:392
  97.0 1.5 copy-done.5
  98.5 3.5 %shard_map.194 = (bf16[8,8,16,1408]{3,2,1,0:T(8,128)(2,1)S(1)}, bf16[32,512]{1,0:T(8,128)(2,1)}) custom-call(s32[2]{0:T(128)S(1)} %pad_add_fusion.place_ref, bf16[8,32,1152]{2,1,0:T(8,128)(2,1)S(1)} %all_to_all.41.got_ref, bf16[8,64,128]{2,1,0:T(8,128)(2,1)S(1)} %all-to-all-done.4.part_ref, bf16[8,48,128]{2,1,0:T(8,128)(2,1)S(1)} %all_to_all.40.got_ref.meta_ref, ...), custom_call_target="tpu_custom_call" | custom-call | tf_op jit(solution)/shard_map/pallas_call | solution.py:42
  102.1 39.9 %all_to_all.42.got_ref = bf16[8,8,16,1408]{3,2,1,0:T(8,128)(2,1)S(1)} all-to-all(bf16[8,8,16,1408]{3,2,1,0:T(8,128)(2,1)S(1)} %get-tuple-element.25), channel_id=1, replica_groups={{0,8,16,24,32,40,48,56},{64,72,80,88,96,104,112,120},{128,136,144,152,1..., dimensions={0} | all-to-all | bytes 5767168 | tf_op jit(solution)/shard_map/all_to_all | solution.py:392
  141.9 0.4 shard_map.195
  142.3 14.4 %all_to_all.43.got_ref = bf16[8,16,1920]{2,1,0:T(8,128)(2,1)S(1)} all-to-all(bf16[8,16,1920]{2,1,0:T(8,128)(2,1)S(1)} %shard_map.195), channel_id=1, replica_groups={{0,64,128,192,256,320,384,448},{8,72,136,200,264,328,392,456},{16,80,14..., dimensions={0} | all-to-all | bytes 983040 | tf_op jit(solution)/shard_map/all_to_all | solution.py:392
  156.7 0.9 shard_map.198
  157.6 4.8 %all-to-all-start.7 = ((bf16[64,16,256]{2,1,0:T(8,128)(2,1)}), bf16[64,16,256]{2,1,0:T(8,128)(2,1)S(1)}, u32[]{:S(2)}, u32[]{:S(2)}) async-start(bf16[64,16,256]{2,1,0:T(8,128)(2,1)} %get-tuple-element.26), calls=%async_computation.7 | async-start | bytes 1048576 | tf_op jit(solution)/shard_map/all_to_all | solution.py:392
  162.5 3.3 %shard_map.196 = bf16[1,128,128]{2,1,0:T(8,128)(2,1)S(1)} custom-call(s32[2]{0:T(128)S(1)} %pad_add_fusion.place_ref, bf16[8,16,1920]{2,1,0:T(8,128)(2,1)S(1)} %all_to_all.43.got_ref, bf16[8,48,128]{2,1,0:T(8,128)(2,1)S(1)} %all_to_all.40.got_ref.meta_ref), custom_call_target="tpu_custom_call" | custom-call | tf_op jit(solution)/shard_map/pallas_call | solution.py:42
  165.7 15.9 %all_gather.3.got_ref = bf16[8,128,128]{2,1,0:T(8,128)(2,1)S(1)} all-gather(bf16[1,128,128]{2,1,0:T(8,128)(2,1)S(1)} %shard_map.196), channel_id=1, replica_groups=mesh['row'=64,'col'=8] {'col'}, dimensions={0}, use_global_device_ids=true | all-gather | bytes 294912 | tf_op jit(solution)/shard_map/all_gather | solution.py:517
  181.6 1.3 shard_map.197
  182.9 0.0 all-to-all-done.7.got_ref
  182.9 1.0 shard_map.199
  (14 shorter events, 0.1 us)
Async XLA Ops:
  0.6 61.9 %copy-start.15 = (s32[32]{0:T(128)S(1)}, s32[32]{0:T(128)}, u32[]{:S(2)}) copy-start(s32[32]{0:T(128)} %param.23) | copy-start | bytes 388
  3.8 29.8 %all-to-all-start = ((bf16[64,16,128]{2,1,0:T(8,128)(2,1)}), bf16[64,16,128]{2,1,0:T(8,128)(2,1)S(1)}, u32[]{:S(2)}, u32[]{:S(2)}) async-start(bf16[64,16,128]{2,1,0:T(8,128)(2,1)} %get-tuple-element.19), calls=%async_computation | async-start | bytes 524288 | tf_op jit(solution)/shard_map/all_to_all | solution.py:392
  33.5 0.7 copy-start.13
  34.3 0.7 copy-start.14
  47.5 1.2 copy-start
  48.8 1.2 copy-start.2
  50.0 1.0 copy-start.8
  51.0 0.7 copy-start.9
  51.7 0.7 copy-start.11
  52.4 34.2 %copy-start.1 = (bf16[1024,512]{1,0:T(8,128)(2,1)S(1)}, bf16[1024,512]{1,0:T(8,128)(2,1)}, u32[]{:S(2)}) copy-start(bf16[1024,512]{1,0:T(8,128)(2,1)} %left_ref.5) | copy-start | bytes 3145732
  52.4 34.2 %copy-start.3 = (bf16[512,1024]{1,0:T(8,128)(2,1)S(1)}, bf16[512,1024]{1,0:T(8,128)(2,1)}, u32[]{:S(2)}) copy-start(bf16[512,1024]{1,0:T(8,128)(2,1)} %right_ref.5) | copy-start | bytes 3145732
  52.4 34.2 %copy-start.10 = (f32[1024]{0:T(1024)S(1)}, f32[1024]{0:T(1024)}, u32[]{:S(2)}) copy-start(f32[1024]{0:T(1024)} %param.27) | copy-start | bytes 12292
  52.4 34.2 %copy-start.12 = (f32[1024]{0:T(1024)S(1)}, f32[1024]{0:T(1024)}, u32[]{:S(2)}) copy-start(f32[1024]{0:T(1024)} %param.26) | copy-start | bytes 12292
  56.1 1.3 copy-start.4
  57.4 0.8 copy-start.6
  58.3 14.5 %all-to-all-start.2 = ((bf16[8,32,1152]{2,1,0:T(8,128)(2,1)}), bf16[8,32,1152]{2,1,0:T(8,128)(2,1)S(1)}, u32[]{:S(2)}, u32[]{:S(2)}) async-start(bf16[8,32,1152]{2,1,0:T(8,128)(2,1)} %copy-done.6), calls=%async_computation.2 | async-start | bytes 1179648 | tf_op jit(solution)/shard_map/all_to_all | solution.py:392
  87.0 0.7 copy-start.7
  87.7 9.3 %all-to-all-start.4 = ((bf16[8,64,128]{2,1,0:T(8,128)(2,1)}), bf16[8,64,128]{2,1,0:T(8,128)(2,1)S(1)}, u32[]{:S(2)}, u32[]{:S(2)}) async-start(bf16[8,64,128]{2,1,0:T(8,128)(2,1)} %copy-done.7), calls=%async_computation.4 | async-start | bytes 262144 | tf_op jit(solution)/shard_map/all_to_all | solution.py:392
  97.0 1.5 copy-start.5
  157.6 25.3 %all-to-all-start.7 = ((bf16[64,16,256]{2,1,0:T(8,128)(2,1)}), bf16[64,16,256]{2,1,0:T(8,128)(2,1)S(1)}, u32[]{:S(2)}, u32[]{:S(2)}) async-start(bf16[64,16,256]{2,1,0:T(8,128)(2,1)} %get-tuple-element.26), calls=%async_computation.7 | async-start | bytes 1048576 | tf_op jit(solution)/shard_map/all_to_all | solution.py:392

commit v3 on v2

v3 whole, which is shorter than its diff:
```python
import functools

import jax
import jax.numpy as jnp
from jax import lax
from jax.experimental import pallas as pl
from jax.experimental.pallas import tpu as pltpu
from jax.sharding import PartitionSpec as P

LOSS_SCALE = 0.015625

F32, BF16, I32 = jnp.float32, jnp.bfloat16, jnp.int32
ROWS, COLS = 64, 8
SIDE = 8
BATCH, HOST = 32, 256
SLOTS, CAP = 256, 8
WIDE, RANK = 1024, 512
TABLES, NAMES, SLICE = 15, 256, 64
BLOCK = 128

NN = ((1,), (0,))
NT = ((1,), (1,))
TN = ((0,), (0,))


def dot(left, right, dims):
    return lax.dot_general(left, right, (dims, ((), ())), preferred_element_type=F32)


def lanes(shape):
    return lax.broadcasted_iota(I32, shape, len(shape) - 1)


def subs(shape):
    return lax.broadcasted_iota(I32, shape, len(shape) - 2)


def one_hot(mask):
    return jnp.where(mask, 1.0, 0.0).astype(BF16)


def call(
    kernel,
    outs,
    *args,
    smem=(),
    far=(),
    far_outs=(),
    scratch=(),
    copies=0,
    vmem=16,
    alias=None,
    cost=None,
):
    single = not isinstance(outs, tuple)
    specs = tuple(
        pl.BlockSpec(memory_space=pltpu.HBM if i in far_outs else pltpu.VMEM)
        for i in range(1 if single else len(outs))
    )
    return pl.pallas_call(
        kernel,
        out_shape=outs,
        in_specs=[
            pl.BlockSpec(
                memory_space=pltpu.SMEM if i in smem else pltpu.HBM if i in far else pltpu.VMEM
            )
            for i in range(len(args))
        ],
        out_specs=specs[0] if single else specs,
        scratch_shapes=[*scratch, *[pltpu.SemaphoreType.DMA] * copies],
        input_output_aliases=alias or {},
        cost_estimate=cost,
        compiler_params=pltpu.CompilerParams(vmem_limit_bytes=vmem * 2**20),
    )(*args)


def begin(*triples):
    copies = [pltpu.make_async_copy(*triple) for triple in triples]
    for copy in copies:
        copy.start()
    return copies


def struct(shape, dtype):
    return jax.ShapeDtypeStruct(shape, dtype)


def route_kernel(count_ref, row_ref, owner_ref, bag_ref, table_ref, send_ref, at_ref):
    eye = subs((SLOTS, SLOTS)) == lanes((SLOTS, SLOTS))

    def column(ref):
        return jnp.sum(jnp.where(eye, ref[...].astype(F32), 0.0), axis=1, keepdims=True)

    row, bag = column(row_ref), column(bag_ref)
    owner = column(owner_ref)
    live = subs((SLOTS, BLOCK)) < count_ref[0]
    hits = jnp.where((owner == lanes((SLOTS, BLOCK)).astype(F32)) & live, 1.0, 0.0)
    before = one_hot(subs((SLOTS, SLOTS)) > lanes((SLOTS, SLOTS)))
    earlier = dot(before, hits.astype(BF16), NN)
    place = jnp.sum(earlier * hits, axis=1, keepdims=True)
    alive = jnp.sum(hits, axis=1, keepdims=True)
    target = jnp.where(alive > 0.5, owner * CAP + place, -1.0)
    at = one_hot(target == lanes((SLOTS, ROWS * CAP)).astype(F32))
    at_ref[...] = at
    looked = dot(one_hot(row == lanes((SLOTS, 1024)).astype(F32)), table_ref[...], NN)
    both = jnp.concatenate(
        [looked.astype(BF16), jnp.broadcast_to(bag, (SLOTS, BLOCK)).astype(BF16)], axis=1
    )
    sent = dot(at, both, TN)
    send_ref[...] = jnp.concatenate(
        [
            sent[:, :BLOCK].reshape(ROWS, CAP, BLOCK),
            sent[:, BLOCK:].reshape(ROWS, CAP, BLOCK),
        ],
        axis=1,
    ).astype(BF16)


def pool_kernel(got_ref, dense_ref, ids_ref, row_ref, out_ref, hot_ref):
    got = got_ref[...].astype(F32)
    data = got[:, :CAP].reshape(ROWS * CAP, BLOCK).astype(BF16)
    bags = got[:, CAP:].reshape(ROWS * CAP, BLOCK)
    hot = one_hot(bags == lanes((ROWS * CAP, BLOCK)).astype(F32))
    hot_ref[...] = hot
    pooled = dot(hot, data, TN)[:BATCH].astype(BF16).astype(F32)
    row = row_ref[...].astype(F32)
    high = jnp.floor(row * (1.0 / 32.0))
    low = row - 32.0 * high
    meta = [part[:, i * BLOCK : (i + 1) * BLOCK] for part in (high, low) for i in range(2)]
    meta = jnp.concatenate(meta + [jnp.zeros((12, BLOCK), F32)], axis=0)
    part = jnp.concatenate([pooled, dense_ref[...].astype(F32)], axis=1)
    ids = ids_ref[...].astype(F32)
    for c in range(COLS):
        top = jnp.concatenate([part[:, c * SLICE : (c + 1) * SLICE], ids], axis=1)
        out_ref[c] = jnp.concatenate([top, meta], axis=0).astype(BF16)


def cross_kernel(
    got_ref,
    tables_far,
    left_far,
    right_far,
    weight_far,
    bias_far,
    out_far,
    x_far,
    counts_far,
    left_end_ref,
    right_end_ref,
    ends_ref,
    tables_ref,
    left_ref,
    right_ref,
    weight_ref,
    bias_ref,
    out_ref,
    x_ref,
    counts_ref,
    *sems,
):
    tables_in, weight_in, bias_in, left_in, right_in = begin(
        (tables_far, tables_ref, sems[0]),
        (weight_far, weight_ref, sems[1]),
        (bias_far, bias_ref, sems[2]),
        (left_far, left_ref, sems[3]),
        (right_far, right_ref, sems[4]),
    )
    ids = got_ref[:, :BATCH, SLICE:].astype(F32).reshape(HOST, SLICE)
    part = got_ref[:, :BATCH, :SLICE].astype(F32).reshape(HOST, SLICE)
    name = lanes((HOST, NAMES)).astype(F32)
    for t in range(TABLES):
        count = jnp.zeros((HOST, NAMES), F32)
        for j in range(4):
            count += jnp.where(ids[:, 4 * t + j : 4 * t + j + 1] == name, 1.0, 0.0)
        counts_ref[t] = count.astype(BF16)
    (counts_out,) = begin((counts_ref, counts_far, sems[5]))
    tables_in.wait()
    pieces = []
    for t in range(TABLES):
        pieces.append(dot(counts_ref[t], tables_ref[t], NT))
        if t % 2:
            x_ref[:, (t // 2) * BLOCK : (t // 2 + 1) * BLOCK] = jnp.concatenate(
                pieces, axis=1
            ).astype(BF16)
            pieces = []
    x_ref[:, WIDE - BLOCK :] = jnp.concatenate(pieces + [part], axis=1).astype(BF16)
    (x_out,) = begin((x_ref, x_far, sems[6]))
    for copy in (weight_in, bias_in, left_in, right_in):
        copy.wait()
    low_rank = jnp.zeros((HOST, RANK), F32)
    back = jnp.zeros((HOST, RANK), F32)
    plain = jnp.zeros((HOST, 1), F32)
    for n in range(4):
        cols = slice(n * 256, (n + 1) * 256)
        x = x_ref[:, cols]
        weighted = x.astype(F32) * weight_ref[:, cols]
        low_rank += dot(x, left_ref[cols, :], NN)
        back += dot(weighted.astype(BF16), right_ref[:, cols], NT)
        plain += jnp.sum(weighted * (bias_ref[:, cols] + 1.0), axis=1, keepdims=True)
    high = plain.astype(BF16).astype(F32)
    lane = lanes((HOST, BLOCK))
    rest = jnp.where(lane == 0, high, jnp.where(lane == 1, plain - high, 0.0))
    out_ref[:, :, :RANK] = low_rank.astype(BF16).reshape(COLS, BATCH, RANK)
    out_ref[:, :, RANK : 2 * RANK] = back.astype(BF16).reshape(COLS, BATCH, RANK)
    out_ref[:, :, 2 * RANK :] = rest.astype(BF16).reshape(COLS, BATCH, BLOCK)
    (out_out,) = begin((out_ref, out_far, sems[7]))
    left_end_ref[...] = left_ref[WIDE - BLOCK :, :]
    right_end_ref[...] = right_ref[:, WIDE - BLOCK :]
    ends_ref[0:1, :] = weight_ref[:, WIDE - BLOCK :]
    ends_ref[1:2, :] = bias_ref[:, WIDE - BLOCK :]
    for copy in (counts_out, x_out, out_out):
        copy.wait()


def residue_kernel(got_ref, label_ref, out_ref):
    total = got_ref[0].astype(F32)
    for c in range(1, COLS):
        total += got_ref[c].astype(F32)
    low_rank = total[:, :RANK].astype(BF16).astype(F32)
    back = total[:, RANK : 2 * RANK]
    plain = total[:, 2 * RANK : 2 * RANK + 1] + total[:, 2 * RANK + 1 : 2 * RANK + 2]
    logits = jnp.sum(low_rank * back, axis=1, keepdims=True) + plain
    eye = subs((BATCH, BATCH)) == lanes((BATCH, BATCH))
    label = jnp.sum(jnp.where(eye, label_ref[...].astype(F32), 0.0), axis=1, keepdims=True)
    residue = (jax.nn.sigmoid(logits) - label) * LOSS_SCALE
    high = residue.astype(BF16).astype(F32)
    lane = lanes((BATCH, BLOCK))
    rest = jnp.where(lane == 0, high, jnp.where(lane == 1, residue - high, 0.0))
    block = jnp.concatenate([low_rank, residue * back, rest], axis=1).astype(BF16)
    for c in range(COLS):
        out_ref[c] = block


def part_kernel(got_ref, left_ref, right_ref, ends_ref, out_far, out_ref, out_sem):
    low_rank = got_ref[:, :, :RANK].reshape(HOST, RANK)
    grad_rank = got_ref[:, :, RANK : 2 * RANK].reshape(HOST, RANK)
    rest = got_ref[:, :, 2 * RANK :].astype(F32).reshape(HOST, BLOCK)
    residue = rest[:, 0:1] + rest[:, 1:2]
    expanded = dot(low_rank, right_ref[...], NN) + ends_ref[1:2, :]
    grad = residue * ends_ref[0:1, :] * (expanded + 1.0) + dot(grad_rank, left_ref[...], NT)
    out_ref[...] = grad.astype(BF16).reshape(COLS, BATCH, BLOCK)
    (copy,) = begin((out_ref, out_far, out_sem))
    copy.wait()


def order(odd, r):
    z, y = r // SIDE, r % SIDE
    return jnp.where(odd == 1, z, y), jnp.where(odd == 1, y, z)


def grads_kernel(
    got_far,
    x_far,
    counts_far,
    left_far,
    right_far,
    weight_far,
    bias_far,
    out_ref,
    vector_ref,
    got_ref,
    x_ref,
    counts_ref,
    left_ref,
    right_ref,
    weight_ref,
    bias_ref,
    band_ref,
    grad_ref,
    *sems,
):
    got_in, right_in, x_in, weight_in, bias_in = begin(
        (got_far, got_ref, sems[0]),
        (right_far, right_ref, sems[1]),
        (x_far, x_ref, sems[2]),
        (weight_far, weight_ref, sems[3]),
        (bias_far, bias_ref, sems[4]),
    )
    odd = lax.axis_index("col") % 2
    for copy in (got_in, right_in, x_in, weight_in, bias_in):
        copy.wait()
    left_in, counts_in = begin(
        (left_far, left_ref, sems[5]),
        (counts_far, counts_ref, sems[6]),
    )
    low_rank = got_ref[:, :, :RANK].reshape(HOST, RANK)
    grad_rank = got_ref[:, :, RANK : 2 * RANK].reshape(HOST, RANK)
    rest = got_ref[:, :, 2 * RANK :].astype(F32).reshape(HOST, BLOCK)
    residue = rest[:, 0:1] + rest[:, 1:2]
    for n in range(4):
        cols = slice(n * 256, (n + 1) * 256)
        x = x_ref[:, cols]
        wide = x.astype(F32)
        expanded = dot(low_rank, right_ref[:, cols], NN) + bias_ref[:, cols]
        vector_ref[1:2, cols] = jnp.sum(
            residue * (wide * expanded + wide), axis=0, keepdims=True
        )
        grad_crossed = residue * weight_ref[:, cols]
        grad_expanded = grad_crossed * wide
        vector_ref[0:1, cols] = jnp.sum(grad_expanded, axis=0, keepdims=True)
        grad_ref[:, cols] = grad_crossed * (expanded + 1.0)
        band_ref[:, cols] = dot(low_rank, grad_expanded.astype(BF16), TN)
        left = dot(x, grad_rank, TN).astype(BF16)
        for i in range(16):
            a, b = order(odd, 16 * n + i)
            out_ref[a, b, :, :RANK] = left[16 * i : 16 * i + 16]
    for r in range(ROWS):
        a, b = order(odd, r)
        band = band_ref[8 * r : 8 * r + 8, :]
        out_ref[a, b, :, RANK : 2 * RANK] = jnp.concatenate(
            [band[:, :RANK], band[:, RANK:]], axis=0
        ).astype(BF16)
    left_in.wait()
    counts_in.wait()
    for n in range(4):
        cols = slice(n * 256, (n + 1) * 256)
        grad = grad_ref[:, cols] + dot(grad_rank, left_ref[cols, :], NT)
        grad = grad.astype(BF16)
        for i in range(4):
            t = 4 * n + i
            if t < TABLES:
                medium = dot(grad[:, i * SLICE : (i + 1) * SLICE], counts_ref[t], TN).astype(BF16)
            else:
                medium = jnp.zeros((SLICE, NAMES), BF16)
            for k in range(4):
                a, b = order(odd, 4 * t + k)
                out_ref[a, b, :, 2 * RANK : SUMS] = medium[16 * k : 16 * k + 16]

def back_kernel(part_ref, hot_ref, vector_ref, _, out_far, sample_ref, out_ref, out_sem):
    odd = lax.axis_index("col") % 2
    grads = jnp.concatenate(
        [part_ref[c].astype(F32)[:, SLICE:] for c in range(COLS)], axis=1
    )
    sample_ref[...] = grads.astype(BF16)
    bag = jnp.concatenate([grads[:, :BLOCK], jnp.zeros((BLOCK - BATCH, BLOCK), F32)], axis=0)
    back = dot(hot_ref[...], bag.astype(BF16), NN).reshape(ROWS, CAP, BLOCK)
    back = jnp.concatenate([back[:, :, :SLICE], back[:, :, SLICE:]], axis=1)
    back = jnp.concatenate([back, back], axis=2)
    blank = jnp.zeros((12, SLICE), F32)
    vectors = []
    for b in range(SIDE):
        pieces = [
            vector_ref[v : v + 1, b * BLOCK + h * SLICE : b * BLOCK + (h + 1) * SLICE]
            for v in range(2)
            for h in range(2)
        ]
        vector = jnp.concatenate(pieces + [blank], axis=0)
        vectors.append(jnp.concatenate([vector, vector], axis=1))
    first = lanes((16, BLOCK)) < SLICE
    for r in range(ROWS):
        a, b = order(odd, r)
        vector = jnp.where(odd == 1, vectors[r % SIDE], vectors[r // SIDE])
        out_ref[a, b] = jnp.where(first, vector, back[r]).astype(BF16)
    (copy,) = begin((out_ref, out_far.at[:, :, :, SUMS:], out_sem))
    copy.wait()


SUMS = 2 * RANK + NAMES


def middle_kernel(got_ref, out_ref):
    vectors = []
    for b in range(SIDE):
        total = got_ref[0, b].astype(F32)
        for a in range(1, SIDE):
            total += got_ref[a, b].astype(F32)
        out_ref[b, :, :SUMS] = total[:, :SUMS].astype(BF16)
        vectors.append(total[:4, SUMS : SUMS + SLICE])
        for a in range(0, SIDE, 2):
            pair = [got_ref[a + i, b, :, SUMS + SLICE :].astype(F32) for i in range(2)]
            at = SUMS + a * SLICE
            out_ref[b, :, at : at + BLOCK] = jnp.concatenate(pair, axis=1).astype(BF16)
    packed = jnp.concatenate(
        [jnp.concatenate(vectors[:4], axis=0), jnp.concatenate(vectors[4:], axis=0)], axis=1
    ).astype(BF16)
    for b in range(SIDE):
        out_ref[b, :, SUMS + 512 :] = packed


def last_kernel(got_ref, left_ref, right_ref, bias_ref, top_ref, medium_ref):
    sums = got_ref[0, :, :SUMS].astype(F32)
    packed = got_ref[0, :, SUMS + 512 :].astype(F32)
    for a in range(1, SIDE):
        sums += got_ref[a, :, :SUMS].astype(F32)
        packed += got_ref[a, :, SUMS + 512 :].astype(F32)
    medium = sums[:, 2 * RANK :].astype(BF16)
    for r in range(ROWS):
        medium_ref[r] = medium
    left_ref[...] = sums[:, :RANK]
    right = sums[:, RANK : 2 * RANK]
    right_ref[...] = jnp.concatenate([right[:8], right[8:]], axis=1)
    for v, ref in ((0, bias_ref), (2, top_ref)):
        pieces = []
        for b in range(SIDE):
            at = (b // 4) * SLICE
            for h in range(2):
                i = 4 * (b % 4) + v + h
                pieces.append(packed[i : i + 1, at : at + SLICE])
        ref[...] = jnp.concatenate(pieces, axis=1)


def slots_kernel(got_ref, at_ref, out_ref, data_scr):
    odd = lax.axis_index("col") % 2
    for second in range(SIDE):
        for first in range(SIDE):
            at = SUMS + first * SLICE
            block = got_ref[second, :, at : at + SLICE].astype(F32)
            r = jnp.where(odd == 1, first * SIDE + second, second * SIDE + first)
            data_scr[r] = jnp.concatenate([block[:CAP], block[CAP:]], axis=1)
    data = data_scr[...].reshape(ROWS * CAP, BLOCK).astype(BF16)
    out_ref[0] = dot(at_ref[...], data, NN).astype(BF16)


def giant_kernel(got_ref, meta_ref, out_ref):
    row = subs((1024, SLOTS)).astype(F32)
    total = jnp.zeros((1024, BLOCK), F32)
    for c in range(COLS):
        meta = meta_ref[c, BATCH : BATCH + 16, :].astype(F32)
        name = jnp.concatenate(
            [meta[i : i + 1] * 32.0 + meta[2 + i : 3 + i] for i in range(2)], axis=1
        )
        total += dot(one_hot(name == row), got_ref[c], NN)
    out_ref[...] = total


def medium_kernel(got_ref, out_ref):
    for t in range(TABLES):
        block = got_ref[4 * t : 4 * t + 4].astype(F32).reshape(SLICE, NAMES)
        out_ref[t] = block


def sides():
    first, second = [], []
    for c in range(COLS):
        for k in range(SIDE):
            along_y = [(k * SIDE + y) * COLS + c for y in range(SIDE)]
            along_z = [(z * SIDE + k) * COLS + c for z in range(SIDE)]
            first.append(along_z if c % 2 else along_y)
            second.append(along_y if c % 2 else along_z)
    return first, second


def swap(value, axis, groups=None):
    return lax.all_to_all(
        value, axis, split_axis=0, concat_axis=0, tiled=True, axis_index_groups=groups
    )


def body(
    giant_table,
    look_row,
    look_owner,
    look_bag,
    look_count,
    medium_tables,
    medium_ids,
    medium_lengths,
    dense_features,
    click_labels,
    cross_left,
    cross_right,
    cross_bias,
    top_weight,
):
    first, second = sides()
    bias, weight = cross_bias.reshape(1, WIDE), top_weight.reshape(1, WIDE)
    live = jnp.arange(4)[None, None, :] < medium_lengths[:, :, None]
    ids = jnp.where(live, medium_ids, NAMES).reshape(BATCH, 4 * TABLES).astype(BF16)
    ids = jnp.pad(ids, ((0, 0), (0, SLICE - 4 * TABLES)))

    look_row = look_row.reshape(1, SLOTS)
    send, at = call(
        route_kernel,
        (struct((ROWS, 2 * CAP, BLOCK), BF16), struct((SLOTS, ROWS * CAP), BF16)),
        look_count,
        look_row,
        look_owner.reshape(1, SLOTS),
        look_bag.reshape(1, SLOTS),
        giant_table,
        smem=(0,),
        vmem=60,
    )
    got = swap(send, "row")
    send, hot = call(
        pool_kernel,
        (struct((COLS, 48, BLOCK), BF16), struct((ROWS * CAP, BLOCK), BF16)),
        got,
        dense_features,
        ids,
        look_row,
    )
    meta = swap(send, "col")
    send, x, counts, left_end, right_end, ends = call(
        cross_kernel,
        (
            struct((COLS, BATCH, 2 * RANK + BLOCK), BF16),
            struct((HOST, WIDE), BF16),
            struct((TABLES, HOST, NAMES), BF16),
            struct((BLOCK, RANK), BF16),
            struct((RANK, BLOCK), BF16),
            struct((2, BLOCK), F32),
        ),
        meta,
        jnp.swapaxes(medium_tables, 1, 2),
        cross_left,
        cross_right,
        weight,
        bias,
        far=(1, 2, 3, 4, 5),
        far_outs=(0, 1, 2),
        scratch=(
            pltpu.VMEM((TABLES, SLICE, NAMES), BF16),
            pltpu.VMEM((WIDE, RANK), BF16),
            pltpu.VMEM((RANK, WIDE), BF16),
            pltpu.VMEM((1, WIDE), F32),
            pltpu.VMEM((1, WIDE), F32),
            pltpu.VMEM((COLS, BATCH, 2 * RANK + BLOCK), BF16),
            pltpu.VMEM((HOST, WIDE), BF16),
            pltpu.VMEM((TABLES, HOST, NAMES), BF16),
        ),
        copies=8,
        vmem=60,
    )
    got = swap(send, "col")
    send = call(
        residue_kernel,
        struct((COLS, BATCH, 2 * RANK + BLOCK), BF16),
        got,
        click_labels.reshape(1, BATCH),
    )
    ranks = swap(send, "col")
    send = call(
        part_kernel,
        struct((COLS, BATCH, BLOCK), BF16),
        ranks,
        left_end,
        right_end,
        ends,
        far_outs=(0,),
        scratch=(pltpu.VMEM((COLS, BATCH, BLOCK), BF16),),
        copies=1,
    )
    parts = swap(send, "col")
    send, vectors = call(
        grads_kernel,
        (struct((SIDE, SIDE, 16, SUMS + BLOCK), BF16), struct((2, WIDE), F32)),
        ranks,
        x,
        counts,
        cross_left,
        cross_right,
        weight,
        bias,
        far=range(7),
        scratch=(
            pltpu.VMEM((COLS, BATCH, 2 * RANK + BLOCK), BF16),
            pltpu.VMEM((HOST, WIDE), BF16),
            pltpu.VMEM((TABLES, HOST, NAMES), BF16),
            pltpu.VMEM((WIDE, RANK), BF16),
            pltpu.VMEM((RANK, WIDE), BF16),
            pltpu.VMEM((1, WIDE), F32),
            pltpu.VMEM((1, WIDE), F32),
            pltpu.VMEM((RANK, WIDE), F32),
            pltpu.VMEM((HOST, WIDE), F32),
        ),
        copies=7,
        vmem=60,
        cost=pl.CostEstimate(flops=3 * 10**9, bytes_accessed=10**7, transcendentals=0),
    )
    send, sample_grads = call(
        back_kernel,
        (
            struct((SIDE, SIDE, 16, SUMS + BLOCK), BF16),
            struct((BATCH, COLS * SLICE), BF16),
        ),
        parts,
        hot,
        vectors,
        send,
        far=(3,),
        far_outs=(0,),
        scratch=(pltpu.VMEM((SIDE, SIDE, 16, BLOCK), BF16),),
        copies=1,
        alias={3: 0},
        vmem=60,
    )
    got = swap(send, ("row", "col"), first)
    send = call(middle_kernel, struct((SIDE, 16, SUMS + 512 + BLOCK), BF16), got)
    got = swap(send, ("row", "col"), second)
    left_grad, right_grad, bias_grad, top_grad, medium = call(
        last_kernel,
        (
            struct((16, RANK), F32),
            struct((8, WIDE), F32),
            struct((1, WIDE), F32),
            struct((1, WIDE), F32),
            struct((ROWS, 16, NAMES), BF16),
        ),
        got,
    )
    medium = swap(medium, "row")
    slots = call(
        slots_kernel,
        struct((1, SLOTS, BLOCK), BF16),
        got,
        at,
        scratch=(pltpu.VMEM((ROWS, CAP, BLOCK), F32),),
    )
    giant_grad = call(
        giant_kernel,
        struct((1024, BLOCK), F32),
        lax.all_gather(slots, "col", axis=0, tiled=True),
        meta,
    )
    medium_grad = jnp.swapaxes(
        call(medium_kernel, struct((TABLES, SLICE, NAMES), F32), medium), 1, 2
    )
    return (
        sample_grads,
        giant_grad,
        medium_grad,
        left_grad,
        right_grad,
        bias_grad.reshape(WIDE),
        top_grad.reshape(WIDE),
    )


def solution(mesh):
    both = P(("row", "col"))
    placed = (
        P("row", None),
        both,
        P(("row", "col"), None),
        both,
        both,
        P(None, None, "col"),
        P(("row", "col"), None, None),
        P(("row", "col"), None),
        P(("row", "col"), None),
        both,
        P("col", None),
        P(None, "col"),
        P("col"),
        P("col"),
    )
    return jax.shard_map(
        body,
        mesh=mesh,
        in_specs=placed,
        out_specs=(
            P(("row", "col"), None),
            P("row", None),
            P(None, None, "col"),
            P(("col", "row"), None),
            P("row", "col"),
            P("col"),
            P("col"),
        ),
        check_vma=False,
    )
```

time: 185 us -> 181 us (0.978)
  blocking collectives: 96.1 us -> 112 us
  waiting for transfers between devices: 27.1 us -> 11.8 us
  local copies, waits for them, and re-layouts: 10.8 us -> 2.87 us
  Pallas kernels: 17.5 us -> 24.4 us
  starting transfers between devices: 30.2 us -> 25.8 us
    all_to_all x4 -> x5, blocking collectives: 80.2 us -> 96.1 us  [swap(): lax.all_to_all(value, axis, split_axis=0, concat_axis=0, tiled=True, axis...]
    all_to_all x4 -> x3, waiting for transfers between devices: 27.1 us -> 11.8 us  [swap(): lax.all_to_all(value, axis, split_axis=0, concat_axis=0, tiled=True, axis...]
    unnamed x32 -> x22, local copies, waits for them, and re-layouts: 10.6 us -> 2.75 us
    pallas_call x11 -> x12, Pallas kernels: 17.5 us -> 24.4 us  [call(): pl.pallas_call(kernel, out_shape=outs, in_specs=[pl.BlockSpec(memory_spac...]
    all_to_all x4 -> x3, starting transfers between devices: 30.2 us -> 25.8 us  [swap(): lax.all_to_all(value, axis, split_axis=0, concat_axis=0, tiled=True, axis...]
  transfers between devices with their start and end apart: 4 -> 3, of which waited for: 3 -> 1; matrix products, arithmetic and copies ran while one was open for 1% -> 0% of each run, Pallas kernels for 3% -> 5%
where the time goes in v3:
time: 181 us; the launch traced here: 179 us
  blocking collectives  112 us (62%)
  starting transfers between devices  25.8 us (14%)
  Pallas kernels  24.4 us (13%)
  waiting for transfers between devices  11.8 us (7%)
  local copies, waits for them, and re-layouts  2.87 us (2%)
    all_to_all x5, blocking collectives, swap(): lax.all_to_all(value, axis, split_axis=0, concat_axis=0, tiled=True, axis...  96.1 us
    all_to_all x3, starting transfers between devices, swap(): lax.all_to_all(value, axis, split_axis=0, concat_axis=0, tiled=True, axis...  25.8 us
    pallas_call x12, Pallas kernels, call(): pl.pallas_call(kernel, out_shape=outs, in_specs=[pl.BlockSpec(memory_spac...  24.4 us
    all_gather x1, blocking collectives, body(): lax.all_gather(slots, 'col', axis=0, tiled=True)  16.1 us
    all_to_all x3, waiting for transfers between devices, swap(): lax.all_to_all(value, axis, split_axis=0, concat_axis=0, tiled=True, axis...  11.8 us
  transfers between devices with their start and end apart: 3, of which 1 were waited for; matrix products, arithmetic and copies ran while one was open for 0% of the time, Pallas kernels for 5%

profile of v3, /device:TPU:1, one launch (start us, length us, event | category | flops | bytes accessed | tf_op | source)
XLA Modules:
  0.0 179.2 jit_solution(8950489082255278541)
XLA Ops:
  0.6 0.0 copy-start.9
  1.3 2.4 %shard_map.189 = (bf16[64,16,128]{2,1,0:T(8,128)(2,1)}, bf16[256,512]{1,0:T(8,128)(2,1)}) custom-call(s32[1]{0:T(128)S(6)} %copy.26.count_ref, s32[1,256]{1,0:T(1,128)} %bitcast.12, s32[1,256]{1,0:T(1,128)} %bitcast.21, s32[1,256]{1,0:T(1,128)} %bitcast.22, bf16[1024,128]{1,0:T(8,128)(2,1)} %table_ref.1), custom_call_target="tpu_custom_call" | custom-call | tf_op jit(solution)/shard_map/pallas_call | solution.py:60
  3.7 17.1 %all-to-all-start = ((bf16[64,16,128]{2,1,0:T(8,128)(2,1)}), bf16[64,16,128]{2,1,0:T(8,128)(2,1)S(1)}, u32[]{:S(2)}, u32[]{:S(2)}) async-start(bf16[64,16,128]{2,1,0:T(8,128)(2,1)} %get-tuple-element.26), calls=%async_computation | async-start | bytes 524288 | tf_op jit(solution)/shard_map/all_to_all | solution.py:444
  20.9 0.8 select_convert_fusion
  21.7 0.1 copy.24
  21.8 11.8 %all-to-all-done.got_ref = bf16[64,16,128]{2,1,0:T(8,128)(2,1)S(1)} async-done(((bf16[64,16,128]{2,1,0:T(8,128)(2,1)}), bf16[64,16,128]{2,1,0:T(8,128)(2,1)S(1)}, u32[]{:S(2)}, u32[]{:S(2)}) %all-to-all-start) | async-done | bytes 262176 | tf_op jit(solution)/shard_map/all_to_all | solution.py:444
  33.5 0.0 copy-start.6
  33.5 0.7 copy-done.6
  34.3 0.0 copy-start.7
  34.3 0.7 copy-done.7
  35.0 0.3 shard_map.190
  35.2 0.0 copy-start.3
  35.2 0.7 copy-done.3
  35.9 12.4 %all_to_all.40.got_ref.meta_ref = bf16[8,48,128]{2,1,0:T(8,128)(2,1)} all-to-all(bf16[8,48,128]{2,1,0:T(8,128)(2,1)S(1)} %get-tuple-element.27), channel_id=1, replica_groups=mesh['row'=64,'col'=8] {'col'}, dimensions={0} | all-to-all | bytes 196608 | tf_op jit(solution)/shard_map/all_to_all | solution.py:444
  48.3 5.8 %shard_map.191 = (bf16[8,32,1152]{2,1,0:T(8,128)(2,1)}, bf16[256,1024]{1,0:T(8,128)(2,1)}, bf16[15,256,256]{2,1,0:T(8,128)(2,1)}, bf16[128,512]{1,0:T(8,128)(2,1...) custom-call(bf16[8,48,128]{2,1,0:T(8,128)(2,1)} %all_to_all.40.got_ref.meta_ref, bf16[15,64,256]{2,1,0:T(8,128)(2,1)} %bitcast.16, ...), custom_call_target="tpu_custom_call" | custom-call | tf_op jit(solution)/shard_map/pallas_call | solution.py:60
  54.1 0.0 copy-start.4
  54.1 0.0 copy-start.5
  54.1 0.0 copy-start.8
  54.1 14.8 %all_to_all.41.got_ref = bf16[8,32,1152]{2,1,0:T(8,128)(2,1)S(1)} all-to-all(bf16[8,32,1152]{2,1,0:T(8,128)(2,1)} %get-tuple-element.28), channel_id=1, replica_groups=mesh['row'=64,'col'=8] {'col'}, dimensions={0} | all-to-all | bytes 1179648 | tf_op jit(solution)/shard_map/all_to_all | solution.py:444
  68.8 0.0 copy-done.9
  68.9 0.3 shard_map.192
  69.2 13.5 %all_to_all.42.got_ref.got_far = bf16[8,32,1152]{2,1,0:T(8,128)(2,1)S(1)} all-to-all(bf16[8,32,1152]{2,1,0:T(8,128)(2,1)S(1)} %shard_map.192), channel_id=1, replica_groups=mesh['row'=64,'col'=8] {'col'}, dimensions={0} | all-to-all | bytes 1179648 | tf_op jit(solution)/shard_map/all_to_all | solution.py:444
  82.6 0.0 copy-start
  82.6 0.0 copy-done.4
  82.6 0.0 copy-done.5
  82.6 0.0 copy-done.8
  82.6 0.9 shard_map.193
  83.6 4.0 %all-to-all-start.4 = ((bf16[8,32,128]{2,1,0:T(8,128)(2,1)}), bf16[8,32,128]{2,1,0:T(8,128)(2,1)S(1)}, u32[]{:S(2)}, u32[]{:S(2)}) async-start(bf16[8,32,128]{2,1,0:T(8,128)(2,1)} %shard_map.193), calls=%async_computation.4 | async-start | bytes 131072 | tf_op jit(solution)/shard_map/all_to_all | solution.py:444
  87.6 0.0 copy-done
  87.6 7.4 %shard_map.194 = (bf16[8,8,16,1408]{3,2,1,0:T(8,128)(2,1)}, f32[2,1024]{1,0:T(2,128)}) custom-call(bf16[8,32,1152]{2,1,0:T(8,128)(2,1)} %copy-done, bf16[256,1024]{1,0:T(8,128)(2,1)} %get-tuple-element.33.x_far, bf16[15,256,256]{2,1,0:T(8,128)(2,1)} %get-tuple-element.34.counts_far, bf16[1024,512]{1,0:T(8,128)(2,1)} %left_far.3, ...), custom_call_target="tpu_custom_call" | custom-call | flops 3000000000 | bytes 10000000 | tf_op jit(solution)/shard_map/pallas_call | solution.py:60
  95.0 0.0 all-to-all-done.4.part_ref
  95.0 0.0 copy-start.10
  95.0 0.6 copy-done.10
  95.6 2.7 %shard_map.195 = (bf16[8,8,16,1408]{3,2,1,0:T(8,128)(2,1)}, bf16[32,512]{1,0:T(8,128)(2,1)}) custom-call(bf16[8,32,128]{2,1,0:T(8,128)(2,1)} %copy-done.10, bf16[512,128]{1,0:T(8,128)(2,1)} %copy-done.3, f32[2,1024]{1,0:T(2,128)} %get-tuple-element.35.vector_ref, bf16[8,8,16,1408]{3,2,1,0:T(8,128)(2,1)} %get-tuple-element.36._), custom_call_target="tpu_custom_call", output_to_operand_aliasing={{0}: (3, {})} | custom-call | tf_op jit(solution)/shard_map/pallas_call | solution.py:60
  98.3 41.3 %all_to_all.43.got_ref = bf16[8,8,16,1408]{3,2,1,0:T(8,128)(2,1)S(1)} all-to-all(bf16[8,8,16,1408]{3,2,1,0:T(8,128)(2,1)} %get-tuple-element.38), channel_id=1, replica_groups={{0,8,16,24,32,40,48,56},{64,72,80,88,96,104,112,120},{128,136,144,152,1..., dimensions={0} | all-to-all | bytes 5767168 | tf_op jit(solution)/shard_map/all_to_all | solution.py:444
  139.6 0.0 copy-start.2
  139.6 0.0 copy-start.1
  139.6 0.4 shard_map.196
  140.0 14.2 %all_to_all.44.got_ref = bf16[8,16,1920]{2,1,0:T(8,128)(2,1)S(1)} all-to-all(bf16[8,16,1920]{2,1,0:T(8,128)(2,1)S(1)} %shard_map.196), channel_id=1, replica_groups={{0,64,128,192,256,320,384,448},{8,72,136,200,264,328,392,456},{16,80,14..., dimensions={0} | all-to-all | bytes 983040 | tf_op jit(solution)/shard_map/all_to_all | solution.py:444
  154.2 0.9 shard_map.199
  155.1 4.6 %all-to-all-start.7 = ((bf16[64,16,256]{2,1,0:T(8,128)(2,1)}), bf16[64,16,256]{2,1,0:T(8,128)(2,1)S(1)}, u32[]{:S(2)}, u32[]{:S(2)}) async-start(bf16[64,16,256]{2,1,0:T(8,128)(2,1)} %get-tuple-element.40), calls=%async_computation.7 | async-start | bytes 1048576 | tf_op jit(solution)/shard_map/all_to_all | solution.py:444
  159.7 0.0 copy-done.2
  159.7 0.3 shard_map.197
  160.1 16.1 %all_gather.3.got_ref = bf16[8,256,128]{2,1,0:T(8,128)(2,1)S(1)} all-gather(bf16[1,256,128]{2,1,0:T(8,128)(2,1)S(1)} %shard_map.197), channel_id=1, replica_groups=mesh['row'=64,'col'=8] {'col'}, dimensions={0}, use_global_device_ids=true | all-gather | bytes 589824 | tf_op jit(solution)/shard_map/all_gather | solution.py:612
  176.2 0.0 copy-done.1
  176.2 2.0 %shard_map.198 = f32[1024,128]{1,0:T(8,128)} custom-call(bf16[8,256,128]{2,1,0:T(8,128)(2,1)S(1)} %all_gather.3.got_ref, bf16[8,48,128]{2,1,0:T(8,128)(2,1)S(1)} %copy-done.1), custom_call_target="tpu_custom_call" | custom-call | tf_op jit(solution)/shard_map/pallas_call | solution.py:60
  178.2 0.0 all-to-all-done.7.got_ref
  178.2 1.0 shard_map.200
  (2 shorter events, 0.0 us)
Async XLA Ops:
  0.6 68.2 %copy-start.9 = (s32[32]{0:T(128)S(1)}, s32[32]{0:T(128)}, u32[]{:S(2)}) copy-start(s32[32]{0:T(128)} %param.23) | copy-start | bytes 388
  3.7 29.8 %all-to-all-start = ((bf16[64,16,128]{2,1,0:T(8,128)(2,1)}), bf16[64,16,128]{2,1,0:T(8,128)(2,1)S(1)}, u32[]{:S(2)}, u32[]{:S(2)}) async-start(bf16[64,16,128]{2,1,0:T(8,128)(2,1)} %get-tuple-element.26), calls=%async_computation | async-start | bytes 524288 | tf_op jit(solution)/shard_map/all_to_all | solution.py:444
  33.5 0.7 copy-start.6
  34.3 0.7 copy-start.7
  35.2 0.7 copy-start.3
  54.1 28.6 %copy-start.4 = (bf16[128,512]{1,0:T(8,128)(2,1)S(1)}, bf16[128,512]{1,0:T(8,128)(2,1)}, u32[]{:S(2)}) copy-start(bf16[128,512]{1,0:T(8,128)(2,1)} %get-tuple-element.29.left_ref) | copy-start | bytes 393220
  54.1 28.6 %copy-start.5 = (bf16[512,128]{1,0:T(8,128)(2,1)S(1)}, bf16[512,128]{1,0:T(8,128)(2,1)}, u32[]{:S(2)}) copy-start(bf16[512,128]{1,0:T(8,128)(2,1)} %get-tuple-element.30.right_ref) | copy-start | bytes 393220
  54.1 28.6 %copy-start.8 = (f32[2,128]{1,0:T(2,128)S(1)}, f32[2,128]{1,0:T(2,128)}, u32[]{:S(2)}) copy-start(f32[2,128]{1,0:T(2,128)} %get-tuple-element.31.ends_ref) | copy-start | bytes 3076
  82.6 5.0 %copy-start = (bf16[8,32,1152]{2,1,0:T(8,128)(2,1)}, bf16[8,32,1152]{2,1,0:T(8,128)(2,1)S(1)}, u32[]{:S(2)}) copy-start(bf16[8,32,1152]{2,1,0:T(8,128)(2,1)S(1)} %all_to_all.42.got_ref.got_far) | copy-start | bytes 1769476
  83.6 11.4 %all-to-all-start.4 = ((bf16[8,32,128]{2,1,0:T(8,128)(2,1)}), bf16[8,32,128]{2,1,0:T(8,128)(2,1)S(1)}, u32[]{:S(2)}, u32[]{:S(2)}) async-start(bf16[8,32,128]{2,1,0:T(8,128)(2,1)} %shard_map.193), calls=%async_computation.4 | async-start | bytes 131072 | tf_op jit(solution)/shard_map/all_to_all | solution.py:444
  95.0 0.6 copy-start.10
  139.6 20.1 %copy-start.2 = (bf16[256,512]{1,0:T(8,128)(2,1)S(1)}, bf16[256,512]{1,0:T(8,128)(2,1)}, u32[]{:S(2)}) copy-start(bf16[256,512]{1,0:T(8,128)(2,1)} %get-tuple-element.39.at_ref) | copy-start | bytes 786436
  139.6 36.6 %copy-start.1 = (bf16[8,48,128]{2,1,0:T(8,128)(2,1)S(1)}, bf16[8,48,128]{2,1,0:T(8,128)(2,1)}, u32[]{:S(2)}) copy-start(bf16[8,48,128]{2,1,0:T(8,128)(2,1)} %all_to_all.40.got_ref.meta_ref) | copy-start | bytes 294916
  155.1 23.1 %all-to-all-start.7 = ((bf16[64,16,256]{2,1,0:T(8,128)(2,1)}), bf16[64,16,256]{2,1,0:T(8,128)(2,1)S(1)}, u32[]{:S(2)}, u32[]{:S(2)}) async-start(bf16[64,16,256]{2,1,0:T(8,128)(2,1)} %get-tuple-element.40), calls=%async_computation.7 | async-start | bytes 1048576 | tf_op jit(solution)/shard_map/all_to_all | solution.py:444

commit v4 on v3

--- a/solution.py
+++ b/solution.py
@@ -51,10 +51,23 @@
     vmem=16,
     alias=None,
     cost=None,
+    pinned=(),
+    free=(),
+    free_outs=(),
 ):
     single = not isinstance(outs, tuple)
+    args = [
+        pltpu.with_memory_space_constraint(arg, pltpu.HBM) if i in pinned else arg
+        for i, arg in enumerate(args)
+    ]
     specs = tuple(
-        pl.BlockSpec(memory_space=pltpu.HBM if i in far_outs else pltpu.VMEM)
+        pl.BlockSpec(
+            memory_space=pl.ANY
+            if i in free_outs
+            else pltpu.HBM
+            if i in far_outs
+            else pltpu.VMEM
+        )
         for i in range(1 if single else len(outs))
     )
     return pl.pallas_call(
@@ -62,7 +75,13 @@
         out_shape=outs,
         in_specs=[
             pl.BlockSpec(
-                memory_space=pltpu.SMEM if i in smem else pltpu.HBM if i in far else pltpu.VMEM
+                memory_space=pltpu.SMEM
+                if i in smem
+                else pl.ANY
+                if i in free
+                else pltpu.HBM
+                if i in far
+                else pltpu.VMEM
             )
             for i in range(len(args))
         ],
@@ -116,23 +135,26 @@
     ).astype(BF16)
 
 
-def pool_kernel(got_ref, dense_ref, ids_ref, row_ref, out_ref, hot_ref):
+def pool_kernel(got_ref, own_ref, meta_ref, out_ref):
     got = got_ref[...].astype(F32)
     data = got[:, :CAP].reshape(ROWS * CAP, BLOCK).astype(BF16)
     bags = got[:, CAP:].reshape(ROWS * CAP, BLOCK)
     hot = one_hot(bags == lanes((ROWS * CAP, BLOCK)).astype(F32))
-    hot_ref[...] = hot
     pooled = dot(hot, data, TN)[:BATCH].astype(BF16).astype(F32)
-    row = row_ref[...].astype(F32)
-    high = jnp.floor(row * (1.0 / 32.0))
-    low = row - 32.0 * high
-    meta = [part[:, i * BLOCK : (i + 1) * BLOCK] for part in (high, low) for i in range(2)]
-    meta = jnp.concatenate(meta + [jnp.zeros((12, BLOCK), F32)], axis=0)
-    part = jnp.concatenate([pooled, dense_ref[...].astype(F32)], axis=1)
-    ids = ids_ref[...].astype(F32)
+    eye = subs((BLOCK, BLOCK)) == lanes((BLOCK, BLOCK))
+    bag_rows = [
+        jnp.sum(jnp.where(eye, bags[i * BLOCK : (i + 1) * BLOCK], 0.0), axis=0, keepdims=True)
+        for i in range(4)
+    ]
+    meta = meta_ref[...].astype(F32)
+    meta = jnp.concatenate([meta[:4], *bag_rows, meta[8:]], axis=0).astype(BF16)
+    own = own_ref[...].astype(F32)
+    part = jnp.concatenate([pooled, own[:, : 3 * BLOCK]], axis=1)
+    ids = own[:, 3 * BLOCK : 3 * BLOCK + SLICE]
     for c in range(COLS):
         top = jnp.concatenate([part[:, c * SLICE : (c + 1) * SLICE], ids], axis=1)
-        out_ref[c] = jnp.concatenate([top, meta], axis=0).astype(BF16)
+        out_ref[c, :BATCH, :] = top.astype(BF16)
+        out_ref[c, BATCH:, :] = meta
 
 
 def cross_kernel(
@@ -142,7 +164,7 @@
     right_far,
     weight_far,
     bias_far,
-    out_far,
+    out_ref,
     x_far,
     counts_far,
     left_end_ref,
@@ -153,7 +175,6 @@
     right_ref,
     weight_ref,
     bias_ref,
-    out_ref,
     x_ref,
     counts_ref,
     *sems,
@@ -203,12 +224,11 @@
     out_ref[:, :, :RANK] = low_rank.astype(BF16).reshape(COLS, BATCH, RANK)
     out_ref[:, :, RANK : 2 * RANK] = back.astype(BF16).reshape(COLS, BATCH, RANK)
     out_ref[:, :, 2 * RANK :] = rest.astype(BF16).reshape(COLS, BATCH, BLOCK)
-    (out_out,) = begin((out_ref, out_far, sems[7]))
     left_end_ref[...] = left_ref[WIDE - BLOCK :, :]
     right_end_ref[...] = right_ref[:, WIDE - BLOCK :]
     ends_ref[0:1, :] = weight_ref[:, WIDE - BLOCK :]
     ends_ref[1:2, :] = bias_ref[:, WIDE - BLOCK :]
-    for copy in (counts_out, x_out, out_out):
+    for copy in (counts_out, x_out):
         copy.wait()
 
 
@@ -249,7 +269,7 @@
 
 
 def grads_kernel(
-    got_far,
+    got_ref,
     x_far,
     counts_far,
     left_far,
@@ -257,8 +277,6 @@
     weight_far,
     bias_far,
     out_ref,
-    vector_ref,
-    got_ref,
     x_ref,
     counts_ref,
     left_ref,
@@ -267,22 +285,20 @@
     bias_ref,
     band_ref,
     grad_ref,
+    vector_ref,
     *sems,
 ):
-    got_in, right_in, x_in, weight_in, bias_in = begin(
-        (got_far, got_ref, sems[0]),
-        (right_far, right_ref, sems[1]),
-        (x_far, x_ref, sems[2]),
-        (weight_far, weight_ref, sems[3]),
-        (bias_far, bias_ref, sems[4]),
+    right_in, x_in, weight_in, bias_in, left_in, counts_in = begin(
+        (right_far, right_ref, sems[0]),
+        (x_far, x_ref, sems[1]),
+        (weight_far, weight_ref, sems[2]),
+        (bias_far, bias_ref, sems[3]),
+        (left_far, left_ref, sems[4]),
+        (counts_far, counts_ref, sems[5]),
     )
     odd = lax.axis_index("col") % 2
-    for copy in (got_in, right_in, x_in, weight_in, bias_in):
+    for copy in (right_in, x_in, weight_in, bias_in):
         copy.wait()
-    left_in, counts_in = begin(
-        (left_far, left_ref, sems[5]),
-        (counts_far, counts_ref, sems[6]),
-    )
     low_rank = got_ref[:, :, :RANK].reshape(HOST, RANK)
     grad_rank = got_ref[:, :, RANK : 2 * RANK].reshape(HOST, RANK)
     rest = got_ref[:, :, 2 * RANK :].astype(F32).reshape(HOST, BLOCK)
@@ -310,32 +326,6 @@
         out_ref[a, b, :, RANK : 2 * RANK] = jnp.concatenate(
             [band[:, :RANK], band[:, RANK:]], axis=0
         ).astype(BF16)
-    left_in.wait()
-    counts_in.wait()
-    for n in range(4):
-        cols = slice(n * 256, (n + 1) * 256)
-        grad = grad_ref[:, cols] + dot(grad_rank, left_ref[cols, :], NT)
-        grad = grad.astype(BF16)
-        for i in range(4):
-            t = 4 * n + i
-            if t < TABLES:
-                medium = dot(grad[:, i * SLICE : (i + 1) * SLICE], counts_ref[t], TN).astype(BF16)
-            else:
-                medium = jnp.zeros((SLICE, NAMES), BF16)
-            for k in range(4):
-                a, b = order(odd, 4 * t + k)
-                out_ref[a, b, :, 2 * RANK : SUMS] = medium[16 * k : 16 * k + 16]
-
-def back_kernel(part_ref, hot_ref, vector_ref, _, out_far, sample_ref, out_ref, out_sem):
-    odd = lax.axis_index("col") % 2
-    grads = jnp.concatenate(
-        [part_ref[c].astype(F32)[:, SLICE:] for c in range(COLS)], axis=1
-    )
-    sample_ref[...] = grads.astype(BF16)
-    bag = jnp.concatenate([grads[:, :BLOCK], jnp.zeros((BLOCK - BATCH, BLOCK), F32)], axis=0)
-    back = dot(hot_ref[...], bag.astype(BF16), NN).reshape(ROWS, CAP, BLOCK)
-    back = jnp.concatenate([back[:, :, :SLICE], back[:, :, SLICE:]], axis=1)
-    back = jnp.concatenate([back, back], axis=2)
     blank = jnp.zeros((12, SLICE), F32)
     vectors = []
     for b in range(SIDE):
@@ -345,14 +335,58 @@
             for h in range(2)
         ]
         vector = jnp.concatenate(pieces + [blank], axis=0)
-        vectors.append(jnp.concatenate([vector, vector], axis=1))
+        vectors.append(jnp.concatenate([vector, jnp.zeros((16, SLICE), F32)], axis=1))
+    out_ref[:, :, :, SUMS:] = jnp.broadcast_to(
+        jnp.stack(vectors, axis=0)[None], (SIDE, SIDE, 16, BLOCK)
+    ).astype(BF16)
+    left_in.wait()
+    counts_in.wait()
+    for n in range(4):
+        cols = slice(n * 256, (n + 1) * 256)
+        grad = grad_ref[:, cols] + dot(grad_rank, left_ref[cols, :], NT)
+        grad = grad.astype(BF16).T
+        for i in range(4):
+            t = 4 * n + i
+            if t < TABLES:
+                medium = dot(grad[i * SLICE : (i + 1) * SLICE], counts_ref[t], NN).astype(BF16)
+            else:
+                medium = jnp.zeros((SLICE, NAMES), BF16)
+            for k in range(4):
+                a, b = order(odd, 4 * t + k)
+                out_ref[a, b, :, 2 * RANK : SUMS] = medium[16 * k : 16 * k + 16]
+
+def back_kernel(
+    part_far, meta_far, sent_far, out_far, sample_far, part_ref, meta_ref, out_ref, sample_ref, *sems
+):
+    del sent_far
+    col = lax.axis_index("col")
+    last = out_far.at[:, :, :, SUMS:]
+    copies = begin(
+        (part_far, part_ref, sems[0]),
+        (meta_far.at[col, BATCH : BATCH + 16], meta_ref, sems[1]),
+        (last, out_ref, sems[2]),
+    )
+    odd = col % 2
+    for copy in copies:
+        copy.wait()
+    grads = jnp.concatenate(
+        [part_ref[c].astype(F32)[:, SLICE:] for c in range(COLS)], axis=1
+    )
+    sample_ref[...] = grads.astype(BF16)
+    sent = begin((sample_ref, sample_far, sems[3]))
+    meta = meta_ref[...].astype(F32)
+    bags = jnp.concatenate([meta[4 + i : 5 + i] for i in range(4)], axis=1)
+    hot = one_hot(bags == subs((BATCH, ROWS * CAP)).astype(F32))
+    back = dot(hot, grads[:, :BLOCK].astype(BF16), TN).reshape(ROWS, CAP, BLOCK)
+    back = jnp.concatenate([back[:, :, :SLICE], back[:, :, SLICE:]], axis=1)
+    back = jnp.concatenate([back, back], axis=2)
     first = lanes((16, BLOCK)) < SLICE
     for r in range(ROWS):
         a, b = order(odd, r)
-        vector = jnp.where(odd == 1, vectors[r % SIDE], vectors[r // SIDE])
-        out_ref[a, b] = jnp.where(first, vector, back[r]).astype(BF16)
-    (copy,) = begin((out_ref, out_far.at[:, :, :, SUMS:], out_sem))
-    copy.wait()
+        out_ref[a, b] = jnp.where(first, out_ref[a, b].astype(F32), back[r]).astype(BF16)
+    sent += begin((out_ref, last, sems[4]))
+    for copy in sent:
+        copy.wait()
 
 
 SUMS = 2 * RANK + NAMES
@@ -411,7 +445,12 @@
     out_ref[0] = dot(at_ref[...], data, NN).astype(BF16)
 
 
-def giant_kernel(got_ref, meta_ref, out_ref):
+def tables_kernel(
+    got_ref, meta_ref, medium_ref, out_far, medium_far, out_ref, wide_ref, out_sem, wide_sem
+):
+    for t in range(TABLES):
+        wide_ref[t] = medium_ref[4 * t : 4 * t + 4].astype(F32).reshape(SLICE, NAMES)
+    copies = begin((wide_ref, medium_far, wide_sem))
     row = subs((1024, SLOTS)).astype(F32)
     total = jnp.zeros((1024, BLOCK), F32)
     for c in range(COLS):
@@ -421,12 +460,9 @@
         )
         total += dot(one_hot(name == row), got_ref[c], NN)
     out_ref[...] = total
-
-
-def medium_kernel(got_ref, out_ref):
-    for t in range(TABLES):
-        block = got_ref[4 * t : 4 * t + 4].astype(F32).reshape(SLICE, NAMES)
-        out_ref[t] = block
+    copies += begin((out_ref, out_far, out_sem))
+    for copy in copies:
+        copy.wait()
 
 
 def sides():
@@ -466,7 +502,10 @@
     bias, weight = cross_bias.reshape(1, WIDE), top_weight.reshape(1, WIDE)
     live = jnp.arange(4)[None, None, :] < medium_lengths[:, :, None]
     ids = jnp.where(live, medium_ids, NAMES).reshape(BATCH, 4 * TABLES).astype(BF16)
-    ids = jnp.pad(ids, ((0, 0), (0, SLICE - 4 * TABLES)))
+    ids = jnp.pad(ids, ((0, 0), (0, BLOCK - 4 * TABLES)))
+    own = jnp.concatenate([dense_features, ids], axis=1)
+    names = jnp.concatenate([look_row // 32, look_row % 32]).astype(BF16).reshape(4, BLOCK)
+    names = jnp.pad(names, ((0, 12), (0, 0)))
 
     look_row = look_row.reshape(1, SLOTS)
     send, at = call(
@@ -481,21 +520,20 @@
         vmem=60,
     )
     got = swap(send, "row")
-    send, hot = call(
+    send = call(
         pool_kernel,
-        (struct((COLS, 48, BLOCK), BF16), struct((ROWS * CAP, BLOCK), BF16)),
+        struct((COLS, 48, BLOCK), BF16),
         got,
-        dense_features,
-        ids,
-        look_row,
+        own,
+        names,
     )
     meta = swap(send, "col")
     send, x, counts, left_end, right_end, ends = call(
         cross_kernel,
         (
-            struct((COLS, BATCH, 2 * RANK + BLOCK), BF16),
-            struct((HOST, WIDE), BF16),
-            struct((TABLES, HOST, NAMES), BF16),
+            pltpu.VMEM((COLS, BATCH, 2 * RANK + BLOCK), BF16),
+            pltpu.HBM((HOST, WIDE), BF16),
+            pltpu.HBM((TABLES, HOST, NAMES), BF16),
             struct((BLOCK, RANK), BF16),
             struct((RANK, BLOCK), BF16),
             struct((2, BLOCK), F32),
@@ -507,19 +545,19 @@
         weight,
         bias,
         far=(1, 2, 3, 4, 5),
-        far_outs=(0, 1, 2),
+        pinned=(1, 2, 3, 4, 5),
+        far_outs=(1, 2),
         scratch=(
             pltpu.VMEM((TABLES, SLICE, NAMES), BF16),
             pltpu.VMEM((WIDE, RANK), BF16),
             pltpu.VMEM((RANK, WIDE), BF16),
             pltpu.VMEM((1, WIDE), F32),
             pltpu.VMEM((1, WIDE), F32),
-            pltpu.VMEM((COLS, BATCH, 2 * RANK + BLOCK), BF16),
             pltpu.VMEM((HOST, WIDE), BF16),
             pltpu.VMEM((TABLES, HOST, NAMES), BF16),
         ),
-        copies=8,
-        vmem=60,
+        copies=7,
+        vmem=32,
     )
     got = swap(send, "col")
     send = call(
@@ -541,9 +579,9 @@
         copies=1,
     )
     parts = swap(send, "col")
-    send, vectors = call(
+    send = call(
         grads_kernel,
-        (struct((SIDE, SIDE, 16, SUMS + BLOCK), BF16), struct((2, WIDE), F32)),
+        pltpu.VMEM((SIDE, SIDE, 16, SUMS + BLOCK), BF16),
         ranks,
         x,
         counts,
@@ -551,9 +589,9 @@
         cross_right,
         weight,
         bias,
-        far=range(7),
+        far=range(1, 7),
+        pinned=range(1, 7),
         scratch=(
-            pltpu.VMEM((COLS, BATCH, 2 * RANK + BLOCK), BF16),
             pltpu.VMEM((HOST, WIDE), BF16),
             pltpu.VMEM((TABLES, HOST, NAMES), BF16),
             pltpu.VMEM((WIDE, RANK), BF16),
@@ -562,27 +600,33 @@
             pltpu.VMEM((1, WIDE), F32),
             pltpu.VMEM((RANK, WIDE), F32),
             pltpu.VMEM((HOST, WIDE), F32),
+            pltpu.VMEM((2, WIDE), F32),
         ),
-        copies=7,
-        vmem=60,
+        copies=6,
+        vmem=40,
         cost=pl.CostEstimate(flops=3 * 10**9, bytes_accessed=10**7, transcendentals=0),
     )
     send, sample_grads = call(
         back_kernel,
         (
-            struct((SIDE, SIDE, 16, SUMS + BLOCK), BF16),
+            pltpu.VMEM((SIDE, SIDE, 16, SUMS + BLOCK), BF16),
             struct((BATCH, COLS * SLICE), BF16),
         ),
         parts,
-        hot,
-        vectors,
+        meta,
         send,
-        far=(3,),
-        far_outs=(0,),
-        scratch=(pltpu.VMEM((SIDE, SIDE, 16, BLOCK), BF16),),
-        copies=1,
-        alias={3: 0},
-        vmem=60,
+        free=(0, 1, 2),
+        far_outs=(1,),
+        free_outs=(0,),
+        scratch=(
+            pltpu.VMEM((COLS, BATCH, BLOCK), BF16),
+            pltpu.VMEM((16, BLOCK), BF16),
+            pltpu.VMEM((SIDE, SIDE, 16, BLOCK), BF16),
+            pltpu.VMEM((BATCH, COLS * SLICE), BF16),
+        ),
+        copies=5,
+        alias={2: 0},
+        vmem=40,
     )
     got = swap(send, ("row", "col"), first)
     send = call(middle_kernel, struct((SIDE, 16, SUMS + 512 + BLOCK), BF16), got)
@@ -606,15 +650,17 @@
         at,
         scratch=(pltpu.VMEM((ROWS, CAP, BLOCK), F32),),
     )
-    giant_grad = call(
-        giant_kernel,
-        struct((1024, BLOCK), F32),
+    giant_grad, medium_grad = call(
+        tables_kernel,
+        (struct((1024, BLOCK), F32), struct((TABLES, SLICE, NAMES), F32)),
         lax.all_gather(slots, "col", axis=0, tiled=True),
         meta,
-    )
-    medium_grad = jnp.swapaxes(
-        call(medium_kernel, struct((TABLES, SLICE, NAMES), F32), medium), 1, 2
-    )
+        medium,
+        far_outs=(0, 1),
+        scratch=(pltpu.VMEM((1024, BLOCK), F32), pltpu.VMEM((TABLES, SLICE, NAMES), F32)),
+        copies=2,
+    )
+    medium_grad = jnp.swapaxes(medium_grad, 1, 2)
     return (
         sample_grads,
         giant_grad,

time: 181 us -> 172 us (0.950)
  Pallas kernels: 24.4 us -> 16.9 us
  blocking collectives: 112 us -> 110 us
  local copies, waits for them, and re-layouts: 2.87 us -> 1.02 us
    pallas_call x12 -> x11, Pallas kernels: 24.4 us -> 16.9 us  [call(): pl.pallas_call(kernel, out_shape=outs, in_specs=[pl.BlockSpec(memory_spac...]
    all_to_all x5, blocking collectives: 96.1 us -> 93.5 us  [swap(): lax.all_to_all(value, axis, split_axis=0, concat_axis=0, tiled=True, axis...]
    unnamed x22 -> x10, local copies, waits for them, and re-layouts: 2.75 us -> 0.91 us
  transfers between devices with their start and end apart: 3 -> 3, of which waited for: 1 -> 2; matrix products, arithmetic and copies ran while one was open for 0% -> 1% of each run, Pallas kernels for 5% -> 2%
where the time goes in v4:
time: 172 us; the launch traced here: 168 us
  blocking collectives  110 us (64%)
  starting transfers between devices  25.8 us (15%)
  Pallas kernels  16.9 us (10%)
  waiting for transfers between devices  11.4 us (7%)
  other arithmetic  2.22 us (1%)
    all_to_all x5, blocking collectives, swap(): lax.all_to_all(value, axis, split_axis=0, concat_axis=0, tiled=True, axis...  93.5 us
    all_to_all x3, starting transfers between devices, swap(): lax.all_to_all(value, axis, split_axis=0, concat_axis=0, tiled=True, axis...  25.8 us
    pallas_call x11, Pallas kernels, call(): pl.pallas_call(kernel, out_shape=outs, in_specs=[pl.BlockSpec(memory_spac...  16.9 us
    all_gather x1, blocking collectives, body(): lax.all_gather(slots, 'col', axis=0, tiled=True)  16.2 us
    all_to_all x3, waiting for transfers between devices, swap(): lax.all_to_all(value, axis, split_axis=0, concat_axis=0, tiled=True, axis...  11.4 us
  transfers between devices with their start and end apart: 3, of which 2 were waited for; matrix products, arithmetic and copies ran while one was open for 1% of the time, Pallas kernels for 2%

profile of v4, /device:TPU:1, one launch (start us, length us, event | category | flops | bytes accessed | tf_op | source)
XLA Modules:
  0.0 168.4 jit_solution(17378456234086755929)
XLA Ops:
  0.6 0.0 copy-start.4
  1.3 2.4 %shard_map.189 = (bf16[64,16,128]{2,1,0:T(8,128)(2,1)}, bf16[256,512]{1,0:T(8,128)(2,1)}) custom-call(s32[1]{0:T(128)S(6)} %copy.26.count_ref, s32[1,256]{1,0:T(1,128)} %bitcast.22, s32[1,256]{1,0:T(1,128)} %bitcast.23, s32[1,256]{1,0:T(1,128)} %bitcast.24, bf16[1024,128]{1,0:T(8,128)(2,1)} %table_ref.1), custom_call_target="tpu_custom_call" | custom-call | tf_op jit(solution)/shard_map/pallas_call | solution.py:73
  3.7 17.1 %all-to-all-start = ((bf16[64,16,128]{2,1,0:T(8,128)(2,1)}), bf16[64,16,128]{2,1,0:T(8,128)(2,1)S(1)}, u32[]{:S(2)}, u32[]{:S(2)}) async-start(bf16[64,16,128]{2,1,0:T(8,128)(2,1)} %get-tuple-element.24), calls=%async_computation | async-start | bytes 524288 | tf_op jit(solution)/shard_map/all_to_all | solution.py:480
  20.9 0.8 select_convert_fusion
  21.7 0.1 copy.24
  21.8 0.7 fusion.8
  22.5 0.7 fusion.1.own_ref
  23.2 10.3 %all-to-all-done.got_ref = bf16[64,16,128]{2,1,0:T(8,128)(2,1)S(1)} async-done(((bf16[64,16,128]{2,1,0:T(8,128)(2,1)}), bf16[64,16,128]{2,1,0:T(8,128)(2,1)S(1)}, u32[]{:S(2)}, u32[]{:S(2)}) %all-to-all-start) | async-done | bytes 262176 | tf_op jit(solution)/shard_map/all_to_all | solution.py:480
  33.5 0.3 shard_map.190
  33.8 12.3 %all_to_all.40.got_ref.meta_far.meta_ref = bf16[8,48,128]{2,1,0:T(8,128)(2,1)S(1)} all-to-all(bf16[8,48,128]{2,1,0:T(8,128)(2,1)S(1)} %shard_map.190), channel_id=1, replica_groups=mesh['row'=64,'col'=8] {'col'}, dimensions={0} | all-to-all | bytes 196608 | tf_op jit(solution)/shard_map/all_to_all | solution.py:480
  46.1 0.0 copy-start
  46.1 3.4 %shard_map.191 = (bf16[8,32,1152]{2,1,0:T(8,128)(2,1)S(1)}, bf16[256,1024]{1,0:T(8,128)(2,1)}, bf16[15,256,256]{2,1,0:T(8,128)(2,1)}, bf16[128,512]{1,0:T(8,128)...) custom-call(bf16[8,48,128]{2,1,0:T(8,128)(2,1)S(1)} %all_to_all.40.got_ref.meta_far.meta_ref, ...), custom_call_target="tpu_custom_call" | custom-call | tf_op jit(solution)/shard_map/pallas_call | solution.py:73
  49.5 13.6 %all_to_all.41.got_ref = bf16[8,32,1152]{2,1,0:T(8,128)(2,1)S(1)} all-to-all(bf16[8,32,1152]{2,1,0:T(8,128)(2,1)S(1)} %get-tuple-element.25), channel_id=1, replica_groups=mesh['row'=64,'col'=8] {'col'}, dimensions={0} | all-to-all | bytes 1179648 | tf_op jit(solution)/shard_map/all_to_all | solution.py:480
  63.1 0.0 copy-done.4
  63.1 0.3 shard_map.192
  63.4 13.5 %all_to_all.42.got_ref = bf16[8,32,1152]{2,1,0:T(8,128)(2,1)S(1)} all-to-all(bf16[8,32,1152]{2,1,0:T(8,128)(2,1)S(1)} %shard_map.192), channel_id=1, replica_groups=mesh['row'=64,'col'=8] {'col'}, dimensions={0} | all-to-all | bytes 1179648 | tf_op jit(solution)/shard_map/all_to_all | solution.py:480
  76.9 0.0 copy-done
  76.9 0.9 shard_map.193
  77.8 4.0 %all-to-all-start.4 = ((bf16[8,32,128]{2,1,0:T(8,128)(2,1)}), bf16[8,32,128]{2,1,0:T(8,128)(2,1)S(1)}, u32[]{:S(2)}, u32[]{:S(2)}) async-start(bf16[8,32,128]{2,1,0:T(8,128)(2,1)} %shard_map.193), calls=%async_computation.4 | async-start | bytes 131072 | tf_op jit(solution)/shard_map/all_to_all | solution.py:480
  81.8 3.7 %shard_map.194.sent_far = bf16[8,8,16,1408]{3,2,1,0:T(8,128)(2,1)S(1)} custom-call(bf16[8,32,1152]{2,1,0:T(8,128)(2,1)S(1)} %all_to_all.42.got_ref, bf16[256,1024]{1,0:T(8,128)(2,1)} %get-tuple-element.29.x_far, bf16[15,256,256]{2,1,0:T(8,128)(2,1)} %get-tuple-element.30.counts_far, bf16[1024,512]{1,0:T(8,128)(2,1)} %left_far.3, ...), custom_call_target="tpu_custom_call" | custom-call | flops 3000000000 | bytes 10000000 | tf_op jit(solution)/shard_map/pallas_call | solution.py:73
  85.6 1.1 all-to-all-done.4.part_far
  86.7 0.0 copy-start.1
  86.7 0.9 copy-done.1
  87.6 1.8 %shard_map.195 = (bf16[8,8,16,1408]{3,2,1,0:T(8,128)(2,1)S(1)}, bf16[32,512]{1,0:T(8,128)(2,1)}) custom-call(bf16[8,32,128]{2,1,0:T(8,128)(2,1)S(1)} %all-to-all-done.4.part_far, bf16[8,48,128]{2,1,0:T(8,128)(2,1)S(1)} %copy-done.1, bf16[8,8,16,1408]{3,2,1,0:T(8,128)(2,1)S(1)} %shard_map.194.sent_far), custom_call_target="tpu_custom_call", output_to_operand_aliasing={{0}: (2, {})} | custom-call | tf_op jit(solution)/shard_map/pallas_call | solution.py:73
  89.4 39.9 %all_to_all.43.got_ref = bf16[8,8,16,1408]{3,2,1,0:T(8,128)(2,1)S(1)} all-to-all(bf16[8,8,16,1408]{3,2,1,0:T(8,128)(2,1)S(1)} %get-tuple-element.32), channel_id=1, replica_groups={{0,8,16,24,32,40,48,56},{64,72,80,88,96,104,112,120},{128,136,144,152,1..., dimensions={0} | all-to-all | bytes 5767168 | tf_op jit(solution)/shard_map/all_to_all | solution.py:480
  129.3 0.0 copy-start.3
  129.3 0.0 copy-start.2
  129.3 0.4 shard_map.196
  129.7 14.3 %all_to_all.44.got_ref = bf16[8,16,1920]{2,1,0:T(8,128)(2,1)S(1)} all-to-all(bf16[8,16,1920]{2,1,0:T(8,128)(2,1)S(1)} %shard_map.196), channel_id=1, replica_groups={{0,64,128,192,256,320,384,448},{8,72,136,200,264,328,392,456},{16,80,14..., dimensions={0} | all-to-all | bytes 983040 | tf_op jit(solution)/shard_map/all_to_all | solution.py:480
  144.0 0.9 shard_map.198
  144.9 4.6 %all-to-all-start.7 = ((bf16[64,16,256]{2,1,0:T(8,128)(2,1)}), bf16[64,16,256]{2,1,0:T(8,128)(2,1)S(1)}, u32[]{:S(2)}, u32[]{:S(2)}) async-start(bf16[64,16,256]{2,1,0:T(8,128)(2,1)} %get-tuple-element.34), calls=%async_computation.7 | async-start | bytes 1048576 | tf_op jit(solution)/shard_map/all_to_all | solution.py:480
  149.5 0.0 copy-done.3
  149.5 0.3 shard_map.197
  149.9 16.2 %all_gather.3.got_ref = bf16[8,256,128]{2,1,0:T(8,128)(2,1)S(1)} all-gather(bf16[1,256,128]{2,1,0:T(8,128)(2,1)S(1)} %shard_map.197), channel_id=1, replica_groups=mesh['row'=64,'col'=8] {'col'}, dimensions={0}, use_global_device_ids=true | all-gather | bytes 589824 | tf_op jit(solution)/shard_map/all_gather | solution.py:656
  166.0 0.0 all-to-all-done.7.medium_ref
  166.1 0.0 copy-done.2
  166.1 2.4 %shard_map.199 = (f32[1024,128]{1,0:T(8,128)}, f32[15,64,256]{2,1,0:T(8,128)}) custom-call(bf16[8,256,128]{2,1,0:T(8,128)(2,1)S(1)} %all_gather.3.got_ref, bf16[8,48,128]{2,1,0:T(8,128)(2,1)S(1)} %copy-done.2, bf16[64,16,256]{2,1,0:T(8,128)(2,1)S(1)} %all-to-all-done.7.medium_ref), custom_call_target="tpu_custom_call" | custom-call | tf_op jit(solution)/shard_map/pallas_call | solution.py:73
  (2 shorter events, 0.0 us)
Async XLA Ops:
  0.6 62.5 %copy-start.4 = (s32[32]{0:T(128)S(1)}, s32[32]{0:T(128)}, u32[]{:S(2)}) copy-start(s32[32]{0:T(128)} %param.23) | copy-start | bytes 388
  3.7 29.8 %all-to-all-start = ((bf16[64,16,128]{2,1,0:T(8,128)(2,1)}), bf16[64,16,128]{2,1,0:T(8,128)(2,1)S(1)}, u32[]{:S(2)}, u32[]{:S(2)}) async-start(bf16[64,16,128]{2,1,0:T(8,128)(2,1)} %get-tuple-element.24), calls=%async_computation | async-start | bytes 524288 | tf_op jit(solution)/shard_map/all_to_all | solution.py:480
  46.1 30.8 %copy-start = (bf16[8,48,128]{2,1,0:T(8,128)(2,1)}, bf16[8,48,128]{2,1,0:T(8,128)(2,1)S(1)}, u32[]{:S(2)}) copy-start(bf16[8,48,128]{2,1,0:T(8,128)(2,1)S(1)} %all_to_all.40.got_ref.meta_far.meta_ref) | copy-start | bytes 294916
  77.8 8.9 %all-to-all-start.4 = ((bf16[8,32,128]{2,1,0:T(8,128)(2,1)}), bf16[8,32,128]{2,1,0:T(8,128)(2,1)S(1)}, u32[]{:S(2)}, u32[]{:S(2)}) async-start(bf16[8,32,128]{2,1,0:T(8,128)(2,1)} %shard_map.193), calls=%async_computation.4 | async-start | bytes 131072 | tf_op jit(solution)/shard_map/all_to_all | solution.py:480
  86.7 0.9 copy-start.1
  129.3 20.3 %copy-start.3 = (bf16[256,512]{1,0:T(8,128)(2,1)S(1)}, bf16[256,512]{1,0:T(8,128)(2,1)}, u32[]{:S(2)}) copy-start(bf16[256,512]{1,0:T(8,128)(2,1)} %get-tuple-element.33.at_ref) | copy-start | bytes 786436
  129.3 36.8 %copy-start.2 = (bf16[8,48,128]{2,1,0:T(8,128)(2,1)S(1)}, bf16[8,48,128]{2,1,0:T(8,128)(2,1)}, u32[]{:S(2)}) copy-start(bf16[8,48,128]{2,1,0:T(8,128)(2,1)} %copy-done) | copy-start | bytes 294916
  144.9 21.2 %all-to-all-start.7 = ((bf16[64,16,256]{2,1,0:T(8,128)(2,1)}), bf16[64,16,256]{2,1,0:T(8,128)(2,1)S(1)}, u32[]{:S(2)}, u32[]{:S(2)}) async-start(bf16[64,16,256]{2,1,0:T(8,128)(2,1)} %get-tuple-element.34), calls=%async_computation.7 | async-start | bytes 1048576 | tf_op jit(solution)/shard_map/all_to_all | solution.py:480

commit v5 on v4

--- a/solution.py
+++ b/solution.py
@@ -170,6 +170,7 @@
     left_end_ref,
     right_end_ref,
     ends_ref,
+    own_ref,
     tables_ref,
     left_ref,
     right_ref,
@@ -224,6 +225,7 @@
     out_ref[:, :, :RANK] = low_rank.astype(BF16).reshape(COLS, BATCH, RANK)
     out_ref[:, :, RANK : 2 * RANK] = back.astype(BF16).reshape(COLS, BATCH, RANK)
     out_ref[:, :, 2 * RANK :] = rest.astype(BF16).reshape(COLS, BATCH, BLOCK)
+    own_ref[...] = got_ref[lax.axis_index("col"), BATCH : BATCH + 16, :]
     left_end_ref[...] = left_ref[WIDE - BLOCK :, :]
     right_end_ref[...] = right_ref[:, WIDE - BLOCK :]
     ends_ref[0:1, :] = weight_ref[:, WIDE - BLOCK :]
@@ -356,15 +358,14 @@
                 out_ref[a, b, :, 2 * RANK : SUMS] = medium[16 * k : 16 * k + 16]
 
 def back_kernel(
-    part_far, meta_far, sent_far, out_far, sample_far, part_ref, meta_ref, out_ref, sample_ref, *sems
+    part_far, meta_ref, sent_far, out_far, sample_far, part_ref, out_ref, sample_ref, *sems
 ):
     del sent_far
     col = lax.axis_index("col")
     last = out_far.at[:, :, :, SUMS:]
     copies = begin(
         (part_far, part_ref, sems[0]),
-        (meta_far.at[col, BATCH : BATCH + 16], meta_ref, sems[1]),
-        (last, out_ref, sems[2]),
+        (last, out_ref, sems[1]),
     )
     odd = col % 2
     for copy in copies:
@@ -373,7 +374,7 @@
         [part_ref[c].astype(F32)[:, SLICE:] for c in range(COLS)], axis=1
     )
     sample_ref[...] = grads.astype(BF16)
-    sent = begin((sample_ref, sample_far, sems[3]))
+    sent = begin((sample_ref, sample_far, sems[2]))
     meta = meta_ref[...].astype(F32)
     bags = jnp.concatenate([meta[4 + i : 5 + i] for i in range(4)], axis=1)
     hot = one_hot(bags == subs((BATCH, ROWS * CAP)).astype(F32))
@@ -384,7 +385,7 @@
     for r in range(ROWS):
         a, b = order(odd, r)
         out_ref[a, b] = jnp.where(first, out_ref[a, b].astype(F32), back[r]).astype(BF16)
-    sent += begin((out_ref, last, sems[4]))
+    sent += begin((out_ref, last, sems[3]))
     for copy in sent:
         copy.wait()
 
@@ -528,7 +529,7 @@
         names,
     )
     meta = swap(send, "col")
-    send, x, counts, left_end, right_end, ends = call(
+    send, x, counts, left_end, right_end, ends, own_meta = call(
         cross_kernel,
         (
             pltpu.VMEM((COLS, BATCH, 2 * RANK + BLOCK), BF16),
@@ -537,6 +538,7 @@
             struct((BLOCK, RANK), BF16),
             struct((RANK, BLOCK), BF16),
             struct((2, BLOCK), F32),
+            pltpu.VMEM((16, BLOCK), BF16),
         ),
         meta,
         jnp.swapaxes(medium_tables, 1, 2),
@@ -613,18 +615,17 @@
             struct((BATCH, COLS * SLICE), BF16),
         ),
         parts,
-        meta,
+        own_meta,
         send,
-        free=(0, 1, 2),
+        free=(0, 2),
         far_outs=(1,),
         free_outs=(0,),
         scratch=(
             pltpu.VMEM((COLS, BATCH, BLOCK), BF16),
-            pltpu.VMEM((16, BLOCK), BF16),
             pltpu.VMEM((SIDE, SIDE, 16, BLOCK), BF16),
             pltpu.VMEM((BATCH, COLS * SLICE), BF16),
         ),
-        copies=5,
+        copies=4,
         alias={2: 0},
         vmem=40,
     )

time: 172 us -> 171 us (level)
  no operation moved by 1% of the time
where the time goes in v5:
time: 171 us; the launch traced here: 168 us
  blocking collectives  110 us (64%)
  starting transfers between devices  25.8 us (15%)
  Pallas kernels  16.9 us (10%)
  waiting for transfers between devices  11.4 us (7%)
  other arithmetic  2.22 us (1%)
    all_to_all x5, blocking collectives, swap(): lax.all_to_all(value, axis, split_axis=0, concat_axis=0, tiled=True, axis...  93.5 us
    all_to_all x3, starting transfers between devices, swap(): lax.all_to_all(value, axis, split_axis=0, concat_axis=0, tiled=True, axis...  25.8 us
    pallas_call x11, Pallas kernels, call(): pl.pallas_call(kernel, out_shape=outs, in_specs=[pl.BlockSpec(memory_spac...  16.9 us
    all_gather x1, blocking collectives, body(): lax.all_gather(slots, 'col', axis=0, tiled=True)  16.1 us
    all_to_all x3, waiting for transfers between devices, swap(): lax.all_to_all(value, axis, split_axis=0, concat_axis=0, tiled=True, axis...  11.4 us
  transfers between devices with their start and end apart: 3, of which 2 were waited for; matrix products, arithmetic and copies ran while one was open for 1% of the time, Pallas kernels for 2%

profile of v5, /device:TPU:1, one launch (start us, length us, event | category | flops | bytes accessed | tf_op | source)
XLA Modules:
  0.0 167.5 jit_solution(11727678319083709970)
XLA Ops:
  0.6 0.0 copy-start.3
  1.3 2.4 %shard_map.189 = (bf16[64,16,128]{2,1,0:T(8,128)(2,1)}, bf16[256,512]{1,0:T(8,128)(2,1)}) custom-call(s32[1]{0:T(128)S(6)} %copy.26.count_ref, s32[1,256]{1,0:T(1,128)} %bitcast.22, s32[1,256]{1,0:T(1,128)} %bitcast.23, s32[1,256]{1,0:T(1,128)} %bitcast.24, bf16[1024,128]{1,0:T(8,128)(2,1)} %table_ref.1), custom_call_target="tpu_custom_call" | custom-call | tf_op jit(solution)/shard_map/pallas_call | solution.py:73
  3.7 17.1 %all-to-all-start = ((bf16[64,16,128]{2,1,0:T(8,128)(2,1)}), bf16[64,16,128]{2,1,0:T(8,128)(2,1)S(1)}, u32[]{:S(2)}, u32[]{:S(2)}) async-start(bf16[64,16,128]{2,1,0:T(8,128)(2,1)} %get-tuple-element.25), calls=%async_computation | async-start | bytes 524288 | tf_op jit(solution)/shard_map/all_to_all | solution.py:481
  20.9 0.8 select_convert_fusion
  21.7 0.1 copy.24
  21.8 0.7 fusion.8
  22.5 0.7 fusion.1.own_ref
  23.2 10.3 %all-to-all-done.got_ref = bf16[64,16,128]{2,1,0:T(8,128)(2,1)S(1)} async-done(((bf16[64,16,128]{2,1,0:T(8,128)(2,1)}), bf16[64,16,128]{2,1,0:T(8,128)(2,1)S(1)}, u32[]{:S(2)}, u32[]{:S(2)}) %all-to-all-start) | async-done | bytes 262176 | tf_op jit(solution)/shard_map/all_to_all | solution.py:481
  33.5 0.3 shard_map.190
  33.8 12.3 %all_to_all.40.got_ref.meta_ref = bf16[8,48,128]{2,1,0:T(8,128)(2,1)S(1)} all-to-all(bf16[8,48,128]{2,1,0:T(8,128)(2,1)S(1)} %shard_map.190), channel_id=1, replica_groups=mesh['row'=64,'col'=8] {'col'}, dimensions={0} | all-to-all | bytes 196608 | tf_op jit(solution)/shard_map/all_to_all | solution.py:481
  46.1 0.0 copy-start
  46.1 3.4 %shard_map.191 = (bf16[8,32,1152]{2,1,0:T(8,128)(2,1)S(1)}, bf16[256,1024]{1,0:T(8,128)(2,1)}, bf16[15,256,256]{2,1,0:T(8,128)(2,1)}, bf16[128,512]{1,0:T(8,128)...) custom-call(bf16[8,48,128]{2,1,0:T(8,128)(2,1)S(1)} %all_to_all.40.got_ref.meta_ref, ...), custom_call_target="tpu_custom_call" | custom-call | tf_op jit(solution)/shard_map/pallas_call | solution.py:73
  49.5 13.6 %all_to_all.41.got_ref = bf16[8,32,1152]{2,1,0:T(8,128)(2,1)S(1)} all-to-all(bf16[8,32,1152]{2,1,0:T(8,128)(2,1)S(1)} %get-tuple-element.26), channel_id=1, replica_groups=mesh['row'=64,'col'=8] {'col'}, dimensions={0} | all-to-all | bytes 1179648 | tf_op jit(solution)/shard_map/all_to_all | solution.py:481
  63.1 0.0 copy-done.3
  63.1 0.3 shard_map.192
  63.4 13.5 %all_to_all.42.got_ref = bf16[8,32,1152]{2,1,0:T(8,128)(2,1)S(1)} all-to-all(bf16[8,32,1152]{2,1,0:T(8,128)(2,1)S(1)} %shard_map.192), channel_id=1, replica_groups=mesh['row'=64,'col'=8] {'col'}, dimensions={0} | all-to-all | bytes 1179648 | tf_op jit(solution)/shard_map/all_to_all | solution.py:481
  76.9 0.0 copy-done
  76.9 0.9 shard_map.193
  77.8 4.0 %all-to-all-start.4 = ((bf16[8,32,128]{2,1,0:T(8,128)(2,1)}), bf16[8,32,128]{2,1,0:T(8,128)(2,1)S(1)}, u32[]{:S(2)}, u32[]{:S(2)}) async-start(bf16[8,32,128]{2,1,0:T(8,128)(2,1)} %shard_map.193), calls=%async_computation.4 | async-start | bytes 131072 | tf_op jit(solution)/shard_map/all_to_all | solution.py:481
  81.8 3.8 %shard_map.194.sent_far = bf16[8,8,16,1408]{3,2,1,0:T(8,128)(2,1)S(1)} custom-call(bf16[8,32,1152]{2,1,0:T(8,128)(2,1)S(1)} %all_to_all.42.got_ref, bf16[256,1024]{1,0:T(8,128)(2,1)} %get-tuple-element.31.x_far, bf16[15,256,256]{2,1,0:T(8,128)(2,1)} %get-tuple-element.32.counts_far, bf16[1024,512]{1,0:T(8,128)(2,1)} %left_far.3, ...), custom_call_target="tpu_custom_call" | custom-call | flops 3000000000 | bytes 10000000 | tf_op jit(solution)/shard_map/pallas_call | solution.py:73
  85.6 1.1 all-to-all-done.4.part_far
  86.7 1.8 %shard_map.195 = (bf16[8,8,16,1408]{3,2,1,0:T(8,128)(2,1)S(1)}, bf16[32,512]{1,0:T(8,128)(2,1)}) custom-call(bf16[8,32,128]{2,1,0:T(8,128)(2,1)S(1)} %all-to-all-done.4.part_far, bf16[16,128]{1,0:T(8,128)(2,1)S(1)} %get-tuple-element.30.meta_ref, bf16[8,8,16,1408]{3,2,1,0:T(8,128)(2,1)S(1)} %shard_map.194.sent_far), custom_call_target="tpu_custom_call", output_to_operand_aliasing={{0}: (2, {})} | custom-call | tf_op jit(solution)/shard_map/pallas_call | solution.py:73
  88.5 39.9 %all_to_all.43.got_ref = bf16[8,8,16,1408]{3,2,1,0:T(8,128)(2,1)S(1)} all-to-all(bf16[8,8,16,1408]{3,2,1,0:T(8,128)(2,1)S(1)} %get-tuple-element.34), channel_id=1, replica_groups={{0,8,16,24,32,40,48,56},{64,72,80,88,96,104,112,120},{128,136,144,152,1..., dimensions={0} | all-to-all | bytes 5767168 | tf_op jit(solution)/shard_map/all_to_all | solution.py:481
  128.4 0.0 copy-start.2
  128.4 0.0 copy-start.1
  128.4 0.4 shard_map.196
  128.8 14.3 %all_to_all.44.got_ref = bf16[8,16,1920]{2,1,0:T(8,128)(2,1)S(1)} all-to-all(bf16[8,16,1920]{2,1,0:T(8,128)(2,1)S(1)} %shard_map.196), channel_id=1, replica_groups={{0,64,128,192,256,320,384,448},{8,72,136,200,264,328,392,456},{16,80,14..., dimensions={0} | all-to-all | bytes 983040 | tf_op jit(solution)/shard_map/all_to_all | solution.py:481
  143.1 0.9 shard_map.198
  144.0 4.6 %all-to-all-start.7 = ((bf16[64,16,256]{2,1,0:T(8,128)(2,1)}), bf16[64,16,256]{2,1,0:T(8,128)(2,1)S(1)}, u32[]{:S(2)}, u32[]{:S(2)}) async-start(bf16[64,16,256]{2,1,0:T(8,128)(2,1)} %get-tuple-element.36), calls=%async_computation.7 | async-start | bytes 1048576 | tf_op jit(solution)/shard_map/all_to_all | solution.py:481
  148.6 0.0 copy-done.2
  148.6 0.3 shard_map.197
  149.0 16.1 %all_gather.3.got_ref = bf16[8,256,128]{2,1,0:T(8,128)(2,1)S(1)} all-gather(bf16[1,256,128]{2,1,0:T(8,128)(2,1)S(1)} %shard_map.197), channel_id=1, replica_groups=mesh['row'=64,'col'=8] {'col'}, dimensions={0}, use_global_device_ids=true | all-gather | bytes 589824 | tf_op jit(solution)/shard_map/all_gather | solution.py:657
  165.1 0.0 all-to-all-done.7.medium_ref
  165.1 0.0 copy-done.1
  165.1 2.4 %shard_map.199 = (f32[1024,128]{1,0:T(8,128)}, f32[15,64,256]{2,1,0:T(8,128)}) custom-call(bf16[8,256,128]{2,1,0:T(8,128)(2,1)S(1)} %all_gather.3.got_ref, bf16[8,48,128]{2,1,0:T(8,128)(2,1)S(1)} %copy-done.1, bf16[64,16,256]{2,1,0:T(8,128)(2,1)S(1)} %all-to-all-done.7.medium_ref), custom_call_target="tpu_custom_call" | custom-call | tf_op jit(solution)/shard_map/pallas_call | solution.py:73
  (2 shorter events, 0.0 us)
Async XLA Ops:
  0.6 62.5 %copy-start.3 = (s32[32]{0:T(128)S(1)}, s32[32]{0:T(128)}, u32[]{:S(2)}) copy-start(s32[32]{0:T(128)} %param.23) | copy-start | bytes 388
  3.7 29.8 %all-to-all-start = ((bf16[64,16,128]{2,1,0:T(8,128)(2,1)}), bf16[64,16,128]{2,1,0:T(8,128)(2,1)S(1)}, u32[]{:S(2)}, u32[]{:S(2)}) async-start(bf16[64,16,128]{2,1,0:T(8,128)(2,1)} %get-tuple-element.25), calls=%async_computation | async-start | bytes 524288 | tf_op jit(solution)/shard_map/all_to_all | solution.py:481
  46.1 30.8 %copy-start = (bf16[8,48,128]{2,1,0:T(8,128)(2,1)}, bf16[8,48,128]{2,1,0:T(8,128)(2,1)S(1)}, u32[]{:S(2)}) copy-start(bf16[8,48,128]{2,1,0:T(8,128)(2,1)S(1)} %all_to_all.40.got_ref.meta_ref) | copy-start | bytes 294916
  77.8 8.9 %all-to-all-start.4 = ((bf16[8,32,128]{2,1,0:T(8,128)(2,1)}), bf16[8,32,128]{2,1,0:T(8,128)(2,1)S(1)}, u32[]{:S(2)}, u32[]{:S(2)}) async-start(bf16[8,32,128]{2,1,0:T(8,128)(2,1)} %shard_map.193), calls=%async_computation.4 | async-start | bytes 131072 | tf_op jit(solution)/shard_map/all_to_all | solution.py:481
  128.4 20.3 %copy-start.2 = (bf16[256,512]{1,0:T(8,128)(2,1)S(1)}, bf16[256,512]{1,0:T(8,128)(2,1)}, u32[]{:S(2)}) copy-start(bf16[256,512]{1,0:T(8,128)(2,1)} %get-tuple-element.35.at_ref) | copy-start | bytes 786436
  128.4 36.8 %copy-start.1 = (bf16[8,48,128]{2,1,0:T(8,128)(2,1)S(1)}, bf16[8,48,128]{2,1,0:T(8,128)(2,1)}, u32[]{:S(2)}) copy-start(bf16[8,48,128]{2,1,0:T(8,128)(2,1)} %copy-done) | copy-start | bytes 294916
  144.0 21.2 %all-to-all-start.7 = ((bf16[64,16,256]{2,1,0:T(8,128)(2,1)}), bf16[64,16,256]{2,1,0:T(8,128)(2,1)S(1)}, u32[]{:S(2)}, u32[]{:S(2)}) async-start(bf16[64,16,256]{2,1,0:T(8,128)(2,1)} %get-tuple-element.36), calls=%async_computation.7 | async-start | bytes 1048576 | tf_op jit(solution)/shard_map/all_to_all | solution.py:481
